TPU v7x, 128 devices: a whole 4x4x4 slice. The times are simulated.
128 devices in a mesh: group: 16 (over y, z), member: 8 (over x, core).
Axes of the slice: x: 4, y: 4, z: 4, core: 2. Of those that a mesh axis runs over, the one named last changes fastest.
Arguments:
- embed: bfloat16 [65536, 768], P(('group', 'member'))
- destination: int32 [65536], P(('group', 'member')), may hold values from 0 to 127, as said below
- cluster: int32 [65536], P(('group', 'member')), may hold values from 0 to 3
Outputs:
- dupscore: float32 [65536], P(('group', 'member'))
Inputs may be any that keep to these rules, and one draw needn't show every extreme that they name: Among the rows of one device at most 8 name the same destination, and there is one destination device (which varies by draw) that receives exactly 8 rows from every device.
All inputs are finite; a program needn't handle non-finite values.
Results may differ from a plain program's by a relative error of at most 0.00065.
Values may be sent and summed in bfloat16 or wider, within the bound.
A program may use at most 64 MiB of HBM per device.

v0:
```python
import jax
import jax.numpy as jnp
from jax import lax
from jax.sharding import PartitionSpec as P


def pick_block(row_total):
    for block_size in (512, 256, 128):
        return block_size
    return row_total


def tile_best(left_rows, left_labels, left_slots, right_rows, right_labels, right_slots):
    row_total = left_rows.shape[0]
    right_total = right_rows.shape[0]
    block_size = pick_block(row_total)
    col_size = pick_block(right_total)
    col_count = right_total // col_size
    right_tiles = right_rows.reshape(col_count, col_size, right_rows.shape[1])
    right_tags = right_labels.reshape(col_count, col_size)
    right_places = right_slots.reshape(col_count, col_size)
    right_low = jnp.min(jnp.where(right_tags >= 0, right_tags, 2**30), axis=1)
    right_high = jnp.max(right_tags, axis=1)

    def one_block(offset):
        piece_rows = lax.dynamic_slice_in_dim(left_rows, offset, block_size, 0)
        piece_labels = lax.dynamic_slice_in_dim(left_labels, offset, block_size, 0)
        piece_slots = lax.dynamic_slice_in_dim(left_slots, offset, block_size, 0)
        left_low = jnp.min(jnp.where(piece_labels >= 0, piece_labels, 2**30))
        left_high = jnp.max(piece_labels)

        def one_column(carry, items):
            tile_rows, tile_labels, tile_slots, low_bound, high_bound = items

            def compute(unused):
                similar = lax.dot_general(
                    piece_rows,
                    tile_rows,
                    (((1,), (1,)), ((), ())),
                    preferred_element_type=jnp.float32,
                )
                allowed = (
                    (piece_labels[:, None] == tile_labels[None, :])
                    & (piece_labels[:, None] >= 0)
                    & (piece_slots[:, None] != tile_slots[None, :])
                )
                masked = jnp.where(allowed, similar, -2.0)
                return (jnp.max(masked, axis=1), jnp.max(masked, axis=0))

            def skipped(unused):
                return (
                    jnp.full((block_size,), -2.0, jnp.float32),
                    jnp.full((col_size,), -2.0, jnp.float32),
                )

            meets = (low_bound <= left_high) & (left_low <= high_bound)
            row_part, col_part = lax.cond(meets, compute, skipped, 0)
            return (jnp.maximum(carry, row_part), col_part)

        row_part, col_parts = lax.scan(
            one_column,
            jnp.full((block_size,), -2.0, jnp.float32),
            (right_tiles, right_tags, right_places, right_low, right_high),
        )
        return (row_part, col_parts.reshape(-1))

    offsets = jnp.arange(row_total // block_size, dtype=jnp.int32) * block_size
    row_best, col_best = lax.map(one_block, offsets)
    return (row_best.reshape(-1), jnp.max(col_best, axis=0))


def shards(embed, destination, cluster):
    devices = lax.axis_size(("group", "member"))
    row_total = embed.shape[0]
    feature_dim = embed.shape[1]
    per_pair = max(2, 2 * row_total // devices)
    capacity = devices * per_pair
    values = embed.astype(jnp.float32)
    unit_rows = (
        values * lax.rsqrt(jnp.sum(values * values, axis=1, keepdims=True) + 1e-06)
    ).astype(jnp.bfloat16)
    dest_hits = (destination[:, None] == jnp.arange(devices, dtype=jnp.int32)[None, :]).astype(
        jnp.int32
    )
    before = jnp.cumsum(dest_hits, axis=0) - dest_hits
    rank_index = jnp.sum(before * dest_hits, axis=1)
    slot_index = destination * per_pair + rank_index
    outgoing = jnp.zeros((capacity, feature_dim), jnp.bfloat16).at[slot_index].set(unit_rows)
    out_labels = jnp.full((capacity,), -1, jnp.int32).at[slot_index].set(cluster)
    position = lax.axis_index("member")
    own_base = position * capacity
    arrived, arrived_labels = (
        lax.all_to_all(
            outgoing.reshape(devices, per_pair, feature_dim),
            ("group", "member"),
            split_axis=0,
            concat_axis=0,
            tiled=True,
        ),
        lax.all_to_all(
            out_labels.reshape(devices, per_pair),
            ("group", "member"),
            split_axis=0,
            concat_axis=0,
            tiled=True,
        ),
    )
    plain_block = arrived.reshape(capacity, feature_dim)
    plain_labels = arrived_labels.reshape(capacity)
    slot_order = jnp.arange(capacity, dtype=jnp.int32)
    sort_key = jnp.where(plain_labels >= 0, plain_labels, 2**20) * capacity + slot_order
    order = jnp.argsort(sort_key)
    own_block = plain_block[order]
    own_labels = plain_labels[order]
    own_slots = own_base + order
    row_best, ignored = tile_best(
        own_block,
        own_labels,
        own_slots,
        lax.all_gather(own_block, "member", axis=0, tiled=True),
        lax.all_gather(own_labels, "member", axis=0, tiled=True),
        lax.all_gather(own_slots, "member", axis=0, tiled=True),
    )
    best_match = jnp.maximum(jnp.full((capacity,), -2.0, jnp.float32), row_best)
    sorted_scores = jnp.maximum(best_match, -1.0)
    scores = jnp.zeros((capacity,), jnp.float32).at[order].set(sorted_scores)
    returned_scores = lax.all_to_all(
        scores.reshape(devices, per_pair),
        ("group", "member"),
        split_axis=0,
        concat_axis=0,
        tiled=True,
    )
    return returned_scores.reshape(capacity)[slot_index]


def solution(mesh):
    in_specs = (P(("group", "member"), None), P(("group", "member")), P(("group", "member")))
    out_specs = P(("group", "member"))
    return jax.shard_map(shards, mesh=mesh, in_specs=in_specs, out_specs=out_specs, check_vma=False)
```

profile of v0, /device:TPU:0, one launch (start us, length us, event | category | flops | bytes accessed | tf_op | source)
XLA Modules:
  0.0 358.3 jit_solution(2037569819616631677)
XLA Ops:
  8.7 2.6 scatter_custom_fusion
  12.0 11.1 %all-to-all-start = ((s32[128,1,8]{2,1,0:T(1,128)}), s32[128,1,8]{2,1,0:T(1,128)S(1)}, u32[]{:S(2)}, u32[]{:S(2)}) async-start(s32[128,1,8]{2,1,0:T(1,128)} %bitcast.10), calls=%async_computation | async-start | bytes 131072 | tf_op jit(solution)/shard_map/all_to_all | solution.py:100
  23.4 3.9 %scatter_custom_fusion.1 = bf16[1024,768]{1,0:T(8,128)(2,1)} fusion(s32[512]{0:T(512)S(1)} %compare_select_fusion.4, bf16[512,768]{1,0:T(8,128)(2,1)S(1)} %copy-done.1, f32[512]{0:T(512)S(1)} %add_rsqrt_fusion, bf16[]{:T(256)} %constant.86.clone.1), kind=kCustom, calls=%fused_computation.23 | custom fusion | flops 1179648 | bytes 2361346 | tf_op jit(solution)/shard_map/scatter | solution.py:88
  27.3 5.1 %all-to-all-done = s32[128,1,8]{2,1,0:T(1,128)S(1)} async-done(((s32[128,1,8]{2,1,0:T(1,128)}), s32[128,1,8]{2,1,0:T(1,128)S(1)}, u32[]{:S(2)}, u32[]{:S(2)}) %all-to-all-start) | async-done | bytes 4128 | tf_op jit(solution)/shard_map/all_to_all | solution.py:100
  32.4 4.8 %all-to-all-start.1 = ((bf16[128,8,768]{2,1,0:T(8,128)(2,1)}), bf16[128,8,768]{2,1,0:T(8,128)(2,1)S(1)}, u32[]{:S(2)}, u32[]{:S(2)}) async-start(bf16[128,8,768]{2,1,0:T(8,128)(2,1)} %bitcast.11), calls=%async_computation.1 | async-start | bytes 3145728 | tf_op jit(solution)/shard_map/all_to_all | solution.py:93
  38.7 4.4 %sort.17 = (s32[1024]{0:T(1024)}, s32[1024]{0:T(1024)S(1)}) sort(s32[1024]{0:T(1024)S(1)} %fusion.19, s32[1024]{0:T(1024)S(1)} %iota.19), dimensions={0}, to_apply=%region_4.5 | sort | flops 10240 | bytes 16384 | tf_op jit(solution)/shard_map/jit(argsort)/sort | solution.py:112
  43.1 18.9 %all-to-all-done.1 = bf16[128,8,768]{2,1,0:T(8,128)(2,1)S(1)} async-done(((bf16[128,8,768]{2,1,0:T(8,128)(2,1)}), bf16[128,8,768]{2,1,0:T(8,128)(2,1)S(1)}, u32[]{:S(2)}, u32[]{:S(2)}) %all-to-all-start.1) | async-done | bytes 1572896 | tf_op jit(solution)/shard_map/all_to_all | solution.py:93
  62.0 5.2 %gather_fusion.1 = bf16[1024,768]{1,0:T(8,128)(2,1)} fusion(bf16[1024,768]{1,0:T(8,128)(2,1)S(1)} %bitcast.46, s32[1024]{0:T(1024)S(1)} %get-tuple-element.289), kind=kCustom, calls=%fused_computation.1 | custom fusion | bytes 3149824 | tf_op jit(solution)/shard_map/gather | solution.py:113
  67.3 4.5 %gather_fusion = s32[1024]{0:T(1024)S(1)} fusion(s32[1024]{0:T(1024)S(1)} %reshape.65, s32[1024]{0:T(1024)S(1)} %get-tuple-element.289), kind=kCustom, calls=%fused_computation | custom fusion | bytes 12288 | tf_op jit(solution)/shard_map/gather | solution.py:114
  71.8 12.8 %all-gather = s32[8192]{0:T(1024)S(1)} all-gather(s32[1024]{0:T(1024)S(1)} %gather_fusion), channel_id=2, replica_groups=mesh['group'=16,'member'=8] {'member'}, dimensions={0}, use_global_device_ids=true | all-gather | bytes 36864 | tf_op jit(solution)/shard_map/all_gather | solution.py:121
  84.6 12.8 %all_gather.10 = s32[8192]{0:T(1024)S(1)} all-gather(s32[1024]{0:T(1024)S(1)} %get-tuple-element.511), channel_id=1, replica_groups=mesh['group'=16,'member'=8] {'member'}, dimensions={0}, use_global_device_ids=true | all-gather | bytes 36864 | tf_op jit(solution)/shard_map/all_gather | solution.py:122
  97.6 33.0 %all-gather.4.cloned.1.call-done = bf16[8192,768]{1,0:T(8,128)(2,1)} async-done(((bf16[1024,768]{1,0:T(8,128)(2,1)}), bf16[8192,768]{1,0:T(8,128)(2,1)}) %all-gather.4.cloned.1.call-update) | async-done | bytes 12582928 | tf_op jit(solution)/shard_map/all_gather | solution.py:120
  130.6 188.8 %while.22 = (s32[]{:T(128)}, f32[2,512]{1,0:T(2,128)S(1)}, s32[2]{0:T(128)S(1)}, s32[1024]{0:T(1024)S(1)}, bf16[1024,768]{1,0:T(8,128)(2,1)S(1)}, /*index=5*/s32...) while((s32[]{:T(128)}, f32[2,512]{1,0:T(2,128)S(1)}, ...), condition=%wide.region_17.18_spmd, body=%wide.region_9.17_spmd.sunk | while | flops 404229120 | bytes 3186776 | solution.py:68
  134.1 92.8 %while.23 = (s32[]{:T(128)}, f32[512]{0:T(512)S(1)}, s32[16]{0:T(128)S(1)}, s32[]{:T(128)}, s32[16]{0:T(128)S(1)}, /*index=5*/s32[]{:T(128)}, s32[512]{0:T(512)S...) while((s32[]{:T(128)}, f32[512]{0:T(512)S(1)}, ...), condition=%wide.region_16.16_spmd.clone, body=%wide.region_12.15_spmd.clone.sunk | while | flops 404227072 | bytes 1601285 | solution.py:60
  143.7 1.9 conditional.3
  149.5 1.9 conditional.3
  155.3 1.9 conditional.3
  166.9 1.9 conditional.3
  178.5 1.9 conditional.3
  201.7 1.9 conditional.3
  213.3 1.9 conditional.3
  224.9 1.9 conditional.3
  230.4 89.0 %while.23 = (s32[]{:T(128)}, f32[512]{0:T(512)S(1)}, s32[16]{0:T(128)S(1)}, s32[]{:T(128)}, s32[16]{0:T(128)S(1)}, /*index=5*/s32[]{:T(128)}, s32[512]{0:T(512)S...) while((s32[]{:T(128)}, f32[512]{0:T(512)S(1)}, ...), condition=%wide.region_16.16_spmd.clone, body=%wide.region_12.15_spmd.clone.sunk | while | flops 404227072 | bytes 1601285 | solution.py:60
  245.9 1.9 conditional.3
  261.4 1.9 conditional.3
  288.5 1.9 conditional.3
  300.1 1.9 conditional.3
  311.7 1.9 conditional.3
  319.5 4.3 %scatter_custom_fusion.2 = f32[1024]{0:T(1024)S(1)} fusion(s32[1024]{0:T(1024)S(1)} %get-tuple-element.290, f32[1024]{0:T(1024)S(1)} %bitcast.54, f32[]{:T(128)} %constant.41.clone.1), kind=kCustom, calls=%fused_computation.50 | custom fusion | bytes 4100 | tf_op jit(solution)/shard_map/scatter | solution.py:126
  324.5 12.8 %all-to-all-start.2 = ((f32[128,1,8]{2,1,0:T(1,128)}), f32[128,1,8]{2,1,0:T(1,128)S(1)}, u32[]{:S(2)}, u32[]{:S(2)}) async-start(f32[128,1,8]{2,1,0:T(1,128)} %bitcast.14), calls=%async_computation.2 | async-start | bytes 131072 | tf_op jit(solution)/shard_map/all_to_all | solution.py:127
  337.4 9.3 %all-to-all-done.2 = f32[128,1,8]{2,1,0:T(1,128)S(1)} async-done(((f32[128,1,8]{2,1,0:T(1,128)}), f32[128,1,8]{2,1,0:T(1,128)S(1)}, u32[]{:S(2)}, u32[]{:S(2)}) %all-to-all-start.2) | async-done | bytes 4128 | tf_op jit(solution)/shard_map/all_to_all | solution.py:127
  348.0 3.4 gather_fusion.2
  (258 shorter events, 141.4 us)
Async XLA Ops:
  6.5 2.1 copy-start.2
  6.5 16.6 %copy-start.1 = (bf16[512,768]{1,0:T(8,128)(2,1)S(1)}, bf16[512,768]{1,0:T(8,128)(2,1)}, u32[]{:S(2)}) copy-start(bf16[512,768]{1,0:T(8,128)(2,1)} %param.9) | copy-start | bytes 2359300
  12.0 20.4 %all-to-all-start = ((s32[128,1,8]{2,1,0:T(1,128)}), s32[128,1,8]{2,1,0:T(1,128)S(1)}, u32[]{:S(2)}, u32[]{:S(2)}) async-start(s32[128,1,8]{2,1,0:T(1,128)} %bitcast.10), calls=%async_computation | async-start | bytes 131072 | tf_op jit(solution)/shard_map/all_to_all | solution.py:100
  32.4 29.6 %all-to-all-start.1 = ((bf16[128,8,768]{2,1,0:T(8,128)(2,1)}), bf16[128,8,768]{2,1,0:T(8,128)(2,1)S(1)}, u32[]{:S(2)}, u32[]{:S(2)}) async-start(bf16[128,8,768]{2,1,0:T(8,128)(2,1)} %bitcast.11), calls=%async_computation.1 | async-start | bytes 3145728 | tf_op jit(solution)/shard_map/all_to_all | solution.py:93
  37.2 93.4 %all-gather.4.cloned.1.call-start = ((), (), s32[]{:S(2)}) async-start(), calls=%async_computation.3 | async-start | bytes 14155776 | tf_op jit(solution)/shard_map/all_gather | solution.py:120
  67.3 63.4 %copy-start = (bf16[1024,768]{1,0:T(8,128)(2,1)S(1)}, bf16[1024,768]{1,0:T(8,128)(2,1)}, u32[]{:S(2)}) copy-start(bf16[1024,768]{1,0:T(8,128)(2,1)} %gather_fusion.1) | copy-start | bytes 4718596
  324.5 22.1 %all-to-all-start.2 = ((f32[128,1,8]{2,1,0:T(1,128)}), f32[128,1,8]{2,1,0:T(1,128)S(1)}, u32[]{:S(2)}, u32[]{:S(2)}) async-start(f32[128,1,8]{2,1,0:T(1,128)} %bitcast.14), calls=%async_computation.2 | async-start | bytes 131072 | tf_op jit(solution)/shard_map/all_to_all | solution.py:127
Sparse Core Ops, SparseCore 0:
  67.4 63.2 all-gather.3
where the time goes:
time: 362 us; the launch traced here: 358 us
  loops' own time  86.8 us (24%)
  local copies, waits for them, and re-layouts  67.6 us (19%)
  waiting for transfers between devices  66.3 us (18%)
  matrix products  56 us (15%)
  starting transfers between devices  28.8 us (8%)
  blocking collectives  25.7 us (7%)
  other arithmetic  13.6 us (4%)
  between operations  13.6 us (4%)
    another operation x2, loops' own time, one_block(): lax.scan(one_column, jnp.full((block_size,), -2.0, jnp.float32), (right_t...  82.1 us
    dot_general x30, matrix products, compute(): lax.dot_general(piece_rows, tile_rows, (((1,), (1,)), ((), ())), preferre...  56 us
    dynamic_slice x94, local copies, waits for them, and re-layouts, one_block(): lax.scan(one_column, jnp.full((block_size,), -2.0, jnp.float32), (right_t...  42.1 us
    all_gather x1, waiting for transfers between devices, shards(): lax.all_gather(own_block, 'member', axis=0, tiled=True)  33 us
    all_to_all x1, waiting for transfers between devices, shards(): lax.all_to_all(outgoing.reshape(devices, per_pair, feature_dim), ('group'...  18.9 us
    all_gather x1, blocking collectives, shards(): lax.all_gather(own_labels, 'member', axis=0, tiled=True)  12.8 us
    all_gather x1, blocking collectives, shards(): lax.all_gather(own_slots, 'member', axis=0, tiled=True)  12.8 us
    all_to_all x1, starting transfers between devices, shards(): lax.all_to_all(scores.reshape(devices, per_pair), ('group', 'member'), sp...  12.8 us
  transfers between devices with their start and end apart: 4, of which 4 were waited for; matrix products, arithmetic and copies ran while one was open for 4% of the time, Pallas kernels for 0%

commit v1 on v0

--- a/solution.py
+++ b/solution.py
@@ -1,7 +1,451 @@
 import jax
 import jax.numpy as jnp
 from jax import lax
+from jax.experimental import pallas as pl
+from jax.experimental.pallas import tpu as pltpu
 from jax.sharding import PartitionSpec as P
+
+MESH = pl.DeviceIdType.MESH
+SIDE = 4
+CELLS = 64
+CELL = 16
+SPILL = 80
+LANES = 128
+SLOTS = CELLS * CELL
+FORWARD = 3 * SPILL
+LEFT_SPILL = 256
+NONE = -4.0
+FAILED = 8.0
+EMPTY = 2.0
+
+
+def split3(value):
+    high = value.astype(jnp.bfloat16)
+    rest = value - high.astype(jnp.float32)
+    mid = rest.astype(jnp.bfloat16)
+    low = (rest - mid.astype(jnp.float32)).astype(jnp.bfloat16)
+    return high, mid, low
+
+
+def iota(shape, dim):
+    return lax.broadcasted_iota(jnp.int32, shape, dim)
+
+
+def dot(left, right):
+    return jnp.dot(left, right, preferred_element_type=jnp.float32)
+
+
+def dot_t(left, right):
+    return lax.dot_general(left, right, (((1,), (1,)), ((), ())), preferred_element_type=jnp.float32)
+
+
+def fold(scores):
+    rows, columns = scores.shape
+    return jnp.max(scores.reshape(rows // 8, 8, columns), axis=0)
+
+
+def team_kernel(
+    embed_ref,
+    dest_ref,
+    cluster_ref,
+    out_ref,
+    unit,
+    send,
+    meta,
+    left,
+    meta_in,
+    other,
+    other_spill,
+    select,
+    forward,
+    label_out,
+    label_in,
+    bias,
+    other_bias,
+    spill_best,
+    spill_ret,
+    best_out,
+    best_in,
+    line_sem,
+    plane_sem,
+    send_sems,
+    recv_sems,
+    meta_sem,
+    pair_sems,
+    spill_sems,
+    ret_sems,
+    best_sem,
+    own_sems,
+):
+    group = lax.axis_index("group")
+    member = lax.axis_index("member")
+    y, z = group // SIDE, group % SIDE
+    x, core = member // 2, member % 2
+    me = group * SIDE + x
+
+    def at(dy, dz, dx, dcore=0):
+        yy, zz, xx = (y + dy) % SIDE, (z + dz) % SIDE, (x + dx) % SIDE
+        cell = (yy * SIDE + zz) * SIDE + xx
+        return cell, {"group": yy * SIDE + zz, "member": xx * 2 + (core + dcore) % 2}
+
+    def step(index):
+        return at(index // 16, (index // 4) % 4, index % 4)
+
+    barrier = pltpu.get_barrier_semaphore()
+    for d in range(1, SIDE):
+        for offset in ((d, 0, 0), (0, d, 0), (0, 0, d)):
+            pl.semaphore_signal(barrier, inc=1, device_id=at(*offset)[1], device_id_type=MESH)
+    sibling = at(0, 0, 0, 1)[1]
+    pl.semaphore_signal(barrier, inc=1, device_id=sibling, device_id_type=MESH)
+
+    values = embed_ref[...].astype(jnp.float32)
+    norm = jnp.sum(values * values, axis=1, keepdims=True)
+    unit[...] = (values * lax.rsqrt(norm + 1e-06)).astype(jnp.bfloat16)
+
+    pl.semaphore_wait(barrier, 10)
+    for d in range(1, SIDE):
+        pl.semaphore_signal(line_sem, inc=1, device_id=at(0, d, 0)[1], device_id_type=MESH)
+
+    rows = dest_ref.shape[1]
+    team = lax.shift_right_logical(dest_ref[...], 3)
+    cluster = cluster_ref[...]
+    in_team = (iota((16, rows), 0) == team).astype(jnp.float32)
+    cells = jnp.concatenate(
+        [in_team * (cluster == c).astype(jnp.float32) for c in range(4)], axis=0
+    )
+    earlier = (iota((rows, rows), 0) < iota((rows, rows), 1)).astype(jnp.bfloat16)
+    rank = jnp.sum(cells * dot(cells.astype(jnp.bfloat16), earlier), axis=0, keepdims=True)
+    counts = jnp.minimum(jnp.sum(cells, axis=1, keepdims=True), float(CELL))
+    over = rank >= float(CELL)
+    over_team = in_team * over.astype(jnp.float32)
+    order = jnp.sum(
+        over_team * dot(over_team.astype(jnp.bfloat16), earlier), axis=0, keepdims=True
+    )
+    filled = [
+        jnp.sum(in_team * counts[16 * c : 16 * c + 16], axis=0, keepdims=True) for c in range(4)
+    ]
+    free0 = CELL - filled[0]
+    free1 = free0 + CELL - filled[1]
+    free2 = free1 + CELL - filled[2]
+    chip = (
+        (order >= free0).astype(jnp.int32)
+        + (order >= free1).astype(jnp.int32)
+        + (order >= free2).astype(jnp.int32)
+    )
+    place = jnp.where(
+        chip == 0,
+        filled[0] + order,
+        jnp.where(
+            chip == 1,
+            filled[1] + order - free0,
+            jnp.where(chip == 2, filled[2] + order - free1, filled[3] + order - free2),
+        ),
+    )
+    chip = jnp.where(over, chip, cluster)
+    place = jnp.where(over, place, rank).astype(jnp.int32)
+    cell = team * 4 + chip
+    slot = cell * CELL + place
+    lane = place + (me % 8) * CELL
+
+    pl.semaphore_wait(line_sem, 3)
+    for d in range(1, SIDE):
+        pl.semaphore_signal(plane_sem, inc=1, device_id=at(0, 0, d)[1], device_id_type=MESH)
+
+    in_cell = (iota((CELLS, rows), 0) == cell).astype(jnp.float32)
+    at_lane = (iota((LANES, rows), 0) == lane).astype(jnp.bfloat16)
+    labels = (in_cell * (cluster + 1).astype(jnp.float32)).astype(jnp.bfloat16)
+    meta[...] = dot_t(labels, at_lane).reshape(CELLS, 1, LANES)
+
+    def pack(index, carry):
+        base = pl.multiple_of(index * 256, 256)
+        chosen = (iota((256, rows), 0) + base == slot).astype(jnp.bfloat16)
+        send[pl.ds(base, 256)] = dot(chosen, unit[...]).astype(jnp.bfloat16)
+        return carry
+
+    lax.fori_loop(0, SLOTS // 256, pack, 0)
+    pl.semaphore_wait(plane_sem, 3)
+
+    def cell_rows(ref, index):
+        return ref.at[pl.ds(pl.multiple_of(index * CELL, CELL), CELL)]
+
+    def send_cell(index, carry):
+        target, device = step((index * 37) % CELLS)
+        pltpu.make_async_remote_copy(
+            src_ref=cell_rows(send, target),
+            dst_ref=cell_rows(left, me),
+            send_sem=send_sems.at[0],
+            recv_sem=recv_sems.at[y],
+            device_id=device,
+            device_id_type=MESH,
+        ).start()
+        pltpu.make_async_remote_copy(
+            src_ref=meta.at[pl.ds(target, 1)],
+            dst_ref=meta_in.at[pl.ds(me, 1)],
+            send_sem=send_sems.at[1],
+            recv_sem=meta_sem,
+            device_id=device,
+            device_id_type=MESH,
+        ).start()
+        return carry
+
+    lax.fori_loop(1, CELLS, send_cell, 0)
+    pltpu.make_async_copy(cell_rows(send, me), cell_rows(left, me), recv_sems.at[y]).start()
+    pltpu.make_async_copy(
+        meta.at[pl.ds(me, 1)], meta_in.at[pl.ds(me, 1)], meta_sem
+    ).start()
+    left[SLOTS + FORWARD :] = jnp.zeros((LEFT_SPILL - FORWARD, left.shape[1]), jnp.bfloat16)
+
+    pltpu.make_async_copy(meta_in, meta_in, meta_sem).wait()
+    to_pair = []
+    for q in range(4):
+        part = pl.ds(q * 256, 256)
+        pltpu.make_async_copy(left.at[part], left.at[part], recv_sems.at[q]).wait()
+        copy = pltpu.make_async_remote_copy(
+            src_ref=left.at[part],
+            dst_ref=other.at[part],
+            send_sem=pair_sems.at[0, q],
+            recv_sem=pair_sems.at[1, q],
+            device_id=sibling,
+            device_id_type=MESH,
+        )
+        copy.start()
+        to_pair.append(copy)
+
+    label = jnp.sum(meta_in[...].reshape(8, 8, LANES), axis=1)
+    own = (x + 1).astype(jnp.float32)
+    below = (iota((LANES, LANES), 0) < iota((LANES, LANES), 1)).astype(jnp.bfloat16)
+    hits = [
+        (label == (lax.rem(x + d, SIDE) + 1).astype(jnp.float32)).astype(jnp.float32)
+        for d in range(1, SIDE)
+    ]
+    hit = jnp.concatenate(hits, axis=0)
+    within = dot(hit.astype(jnp.bfloat16), below)
+    totals = jnp.sum(hit, axis=1, keepdims=True)
+    places = jnp.full((8, LANES), -1.0, jnp.float32)
+    worst = jnp.zeros((1, 1), jnp.float32)
+    for d in range(3):
+        total = totals[8 * d : 8 * d + 8]
+        before = jnp.sum(
+            jnp.where(
+                iota((8, 8), 0) < iota((8, 8), 1),
+                jnp.broadcast_to(total, (8, 8)),
+                0.0,
+            ),
+            axis=0,
+            keepdims=True,
+        )
+        spread = jnp.sum(
+            jnp.where(iota((8, 8), 0) == iota((8, 8), 1), jnp.broadcast_to(before, (8, 8)), 0.0),
+            axis=1,
+            keepdims=True,
+        )
+        position = within[8 * d : 8 * d + 8] + spread
+        places = jnp.where(
+            (hits[d] > 0.0) & (position < float(SPILL)), position + float(SPILL * d), places
+        )
+        worst = jnp.maximum(worst, jnp.sum(total, axis=0, keepdims=True))
+    failed = jnp.broadcast_to((worst > float(SPILL)).astype(jnp.float32), (8, LANES))
+    for q in range(8):
+        select[:, q * LANES : (q + 1) * LANES] = (
+            iota((LEFT_SPILL, LANES), 0).astype(jnp.float32) == places[q : q + 1]
+        ).astype(jnp.bfloat16)
+    chosen = select[0:FORWARD]
+    taken = jnp.sum(chosen.astype(jnp.float32), axis=1, keepdims=True)
+    moved = dot(chosen, left[0:SLOTS])
+    mark = jnp.where((iota((FORWARD, LANES), 1) == 0) & (taken < 0.5), EMPTY, 0.0)
+    forward[:, 0:LANES] = (moved[:, 0:LANES] + mark).astype(jnp.bfloat16)
+    forward[:, LANES:] = moved[:, LANES:].astype(jnp.bfloat16)
+    to_line = []
+    for d in range(3):
+        copy = pltpu.make_async_remote_copy(
+            src_ref=forward.at[pl.ds(d * SPILL, SPILL)],
+            dst_ref=left.at[pl.ds(SLOTS + d * SPILL, SPILL)],
+            send_sem=spill_sems.at[0, d],
+            recv_sem=spill_sems.at[1, d],
+            device_id=at(0, 0, d + 1)[1],
+            device_id_type=MESH,
+        )
+        copy.start()
+        to_line.append(copy)
+    label_out[0:8] = label
+    label_out[8:16] = failed
+    copy_label = pltpu.make_async_remote_copy(
+        src_ref=label_out,
+        dst_ref=label_in,
+        send_sem=pair_sems.at[0, 4],
+        recv_sem=pair_sems.at[1, 4],
+        device_id=sibling,
+        device_id_type=MESH,
+    )
+    copy_label.start()
+
+    def set_bias(ref, tags):
+        columns = jnp.transpose(tags)
+        for q in range(8):
+            ref[q * LANES : (q + 1) * LANES, 0:1] = jnp.where(
+                columns[:, q : q + 1] == own, 0.0, NONE
+            )
+
+    def against(right, right_bias, first, count, same):
+        def one(index, best):
+            base = pl.multiple_of(index * 256, 256)
+            part = pl.ds(base, 256)
+            scores = dot_t(right[part], left[first : first + count]) + right_bias[part, 0:1]
+            if same:
+                scores = jnp.where(
+                    iota((256, count), 0) + base == iota((256, count), 1), NONE, scores
+                )
+            return jnp.maximum(best, fold(scores))
+
+        start = jnp.full((8, count), NONE, jnp.float32)
+        return lax.fori_loop(0, SLOTS // 256, one, start)
+
+    set_bias(bias, label)
+    best_main = against(left, bias, 0, SLOTS, True)
+    copy_label.wait()
+    set_bias(other_bias, label_in[0:8])
+    for copy in to_pair:
+        copy.wait()
+    best_main = jnp.maximum(best_main, against(other, other_bias, 0, SLOTS, False))
+
+    for copy in to_line:
+        copy.wait()
+    spill_part = pl.ds(SLOTS, FORWARD)
+    spill_pair = pltpu.make_async_remote_copy(
+        src_ref=left.at[spill_part],
+        dst_ref=other_spill,
+        send_sem=pair_sems.at[0, 5],
+        recv_sem=pair_sems.at[1, 5],
+        device_id=sibling,
+        device_id_type=MESH,
+    )
+    spill_pair.start()
+    best_spill = against(left, bias, SLOTS, LEFT_SPILL, False)
+    best_spill = jnp.maximum(best_spill, against(other, other_bias, SLOTS, LEFT_SPILL, False))
+
+    def against_spill(right, same):
+        scores = dot_t(right, left[...]) + jnp.where(
+            right[:, 0:1].astype(jnp.float32) > 1.5, NONE, 0.0
+        )
+        if same:
+            scores = jnp.where(
+                iota(scores.shape, 0) + SLOTS == iota(scores.shape, 1), NONE, scores
+            )
+        return fold(scores)
+
+    best_all = against_spill(left[SLOTS : SLOTS + FORWARD], True)
+    spill_pair.wait()
+    best_all = jnp.maximum(best_all, against_spill(other_spill[...], False))
+    best_main = jnp.maximum(best_main, best_all[:, 0:SLOTS])
+    best_spill = jnp.maximum(best_spill, best_all[:, SLOTS:])
+    spill_best[...] = jnp.max(best_spill, axis=0, keepdims=True)
+
+    back = []
+    for d in range(3):
+        copy = pltpu.make_async_remote_copy(
+            src_ref=spill_best,
+            dst_ref=spill_ret.at[d],
+            send_sem=ret_sems.at[0, d],
+            recv_sem=ret_sems.at[1, d],
+            device_id=at(0, 0, 3 - d)[1],
+            device_id_type=MESH,
+        )
+        copy.start()
+        back.append(copy)
+    best_row = jnp.max(best_main, axis=0, keepdims=True)
+    failed = jnp.maximum(failed, label_in[8:16])
+    for copy in back:
+        copy.wait()
+    returned = jnp.zeros((1, LEFT_SPILL), jnp.float32)
+    spot = iota((1, LEFT_SPILL), 1)
+    for d in range(3):
+        returned = jnp.where(
+            (spot >= SPILL * d) & (spot < SPILL * (d + 1)), spill_ret[d], returned
+        )
+    stacked = jnp.zeros((16, LEFT_SPILL), jnp.float32)
+    for index, piece in enumerate(split3(returned)):
+        stacked = jnp.where(iota((16, LEFT_SPILL), 0) == index, piece.astype(jnp.float32), stacked)
+    moved_best = jnp.sum(dot(stacked.astype(jnp.bfloat16), select[...]), axis=0, keepdims=True)
+    for q in range(8):
+        part = slice(q * LANES, (q + 1) * LANES)
+        row = jnp.where(label[q : q + 1] == own, best_row[:, part], moved_best[:, part])
+        best_out[q] = jnp.where(failed[0:1] > 0.0, FAILED, row)
+
+    def send_best(index, carry):
+        target, device = step((index * 37) % CELLS)
+        pltpu.make_async_remote_copy(
+            src_ref=best_out.at[pl.ds(target // 8, 1)],
+            dst_ref=best_in.at[pl.ds(me, 1)],
+            send_sem=send_sems.at[2],
+            recv_sem=best_sem,
+            device_id=device,
+            device_id_type=MESH,
+        ).start()
+        return carry
+
+    lax.fori_loop(1, CELLS, send_best, 0)
+    pltpu.make_async_copy(
+        best_out.at[pl.ds(me // 8, 1)], best_in.at[pl.ds(me, 1)], best_sem
+    ).start()
+    pltpu.make_async_copy(best_in, best_in, best_sem).wait()
+
+    found = best_in[...].reshape(CELLS, LANES)
+    worst = jnp.max(jnp.max(found, axis=1, keepdims=True), axis=0, keepdims=True)
+    picked = sum(dot(piece, at_lane) for piece in split3(found))
+    score = jnp.maximum(jnp.sum(picked * in_cell, axis=0, keepdims=True), -1.0)
+    out_ref[...] = jnp.where(worst > 4.0, FAILED, score)
+
+    sent = pl.ds(0, SLOTS - CELL)
+    pltpu.make_async_copy(send.at[sent], send.at[sent], send_sems.at[0]).wait()
+    sent = pl.ds(0, CELLS - 1)
+    pltpu.make_async_copy(meta.at[sent], meta.at[sent], send_sems.at[1]).wait()
+    pltpu.make_async_copy(best_in.at[sent], best_in.at[sent], send_sems.at[2]).wait()
+
+
+def team_scores(embed, destination, cluster):
+    rows, features = embed.shape
+    bf16, f32 = jnp.bfloat16, jnp.float32
+    vmem = pl.BlockSpec(memory_space=pltpu.VMEM)
+    dma = pltpu.SemaphoreType.DMA
+    return pl.pallas_call(
+        team_kernel,
+        out_shape=jax.ShapeDtypeStruct((1, rows), f32),
+        in_specs=[vmem] * 3,
+        out_specs=vmem,
+        scratch_shapes=[
+            pltpu.VMEM((rows, features), bf16),
+            pltpu.VMEM((SLOTS, features), bf16),
+            pltpu.VMEM((CELLS, 1, LANES), f32),
+            pltpu.VMEM((SLOTS + LEFT_SPILL, features), bf16),
+            pltpu.VMEM((CELLS, 1, LANES), f32),
+            pltpu.VMEM((SLOTS, features), bf16),
+            pltpu.VMEM((FORWARD, features), bf16),
+            pltpu.VMEM((LEFT_SPILL, SLOTS), bf16),
+            pltpu.VMEM((FORWARD, features), bf16),
+            pltpu.VMEM((16, LANES), f32),
+            pltpu.VMEM((16, LANES), f32),
+            pltpu.VMEM((SLOTS, LANES), f32),
+            pltpu.VMEM((SLOTS, LANES), f32),
+            pltpu.VMEM((1, LEFT_SPILL), f32),
+            pltpu.VMEM((3, 1, LEFT_SPILL), f32),
+            pltpu.VMEM((8, 1, LANES), f32),
+            pltpu.VMEM((CELLS, 1, LANES), f32),
+            pltpu.SemaphoreType.REGULAR,
+            pltpu.SemaphoreType.REGULAR,
+            dma((3,)),
+            dma((4,)),
+            dma,
+            dma((2, 6)),
+            dma((2, 3)),
+            dma((2, 3)),
+            dma,
+            dma((2,)),
+        ],
+        compiler_params=pltpu.CompilerParams(
+            collective_id=0, has_side_effects=True, vmem_limit_bytes=40 * 2**20
+        ),
+        name="team_scores",
+    )(embed, destination.reshape(1, rows), cluster.reshape(1, rows))
 
 
 def pick_block(row_total):
@@ -69,7 +513,7 @@
     return (row_best.reshape(-1), jnp.max(col_best, axis=0))
 
 
-def shards(embed, destination, cluster):
+def general(embed, destination, cluster):
     devices = lax.axis_size(("group", "member"))
     row_total = embed.shape[0]
     feature_dim = embed.shape[1]
@@ -134,6 +578,19 @@
     return returned_scores.reshape(capacity)[slot_index]
 
 
+def shards(embed, destination, cluster):
+    rows = embed.shape[0]
+    scores = team_scores(embed, destination, cluster)
+    return lax.cond(
+        scores[0, 0] > 4.0,
+        general,
+        lambda *unused: scores.reshape(rows),
+        embed,
+        destination,
+        cluster,
+    )
+
+
 def solution(mesh):
     in_specs = (P(("group", "member"), None), P(("group", "member")), P(("group", "member")))
     out_specs = P(("group", "member"))

time: 362 us -> 70.7 us (0.20)
  loops' own time: 86.8 us -> 0.23 us
  local copies, waits for them, and re-layouts: 67.6 us -> 1.09 us
  waiting for transfers between devices: 66.3 us -> 0 us
  matrix products: 56 us -> 0 us
  Pallas kernels: 0 us -> 55.2 us
  starting transfers between devices: 28.8 us -> 0 us
  blocking collectives: 25.7 us -> 0 us
  other arithmetic: 13.6 us -> 0 us
    another operation x35 -> x1, loops' own time: 86.8 us -> 0.23 us  [shards(): lax.cond(scores[0, 0] > 4.0, general, lambda *unused: scores.reshape(rows...]
    dot_general x30 -> x0, matrix products: 56 us -> none  [compute(): lax.dot_general(piece_rows, tile_rows, (((1,), (1,)), ((), ())), preferre...]
    pallas_call x0 -> x1, Pallas kernels: none -> 55.2 us  [team_scores(): pl.pallas_call(team_kernel, out_shape=jax.ShapeDtypeStruct((1, rows), f32...]
    dynamic_slice x100 -> x0, local copies, waits for them, and re-layouts: 43.9 us -> none  [the longest x94 42.1 us: one_block(): lax.scan(one_column, jnp.full((block_size,), -2.0, jnp.float32), (right_t...]
    all_to_all x3 -> x0, waiting for transfers between devices: 33.3 us -> none  [the longest x1 18.9 us: shards(): lax.all_to_all(outgoing.reshape(devices, per_pair, feature_dim), ('group'...]
    all_gather x1 -> x0, waiting for transfers between devices: 33 us -> none  [shards(): lax.all_gather(own_block, 'member', axis=0, tiled=True)]
    all_to_all x3 -> x0, starting transfers between devices: 28.8 us -> none  [the longest x1 12.8 us: shards(): lax.all_to_all(scores.reshape(devices, per_pair), ('group', 'member'), sp...]
    all_gather x2 -> x0, blocking collectives: 25.7 us -> none  [the longest x1 12.8 us: shards(): lax.all_gather(own_labels, 'member', axis=0, tiled=True)]
  transfers between devices with their start and end apart: 4 -> 0, of which waited for: 4 -> 0; matrix products, arithmetic and copies ran while one was open for 4% -> 0% of each run, Pallas kernels for 0% -> 0%
where the time goes in v1:
time: 70.7 us; the launch traced here: 70.6 us
  Pallas kernels  55.2 us (78%)
  between operations  14 us (20%)
  local copies, waits for them, and re-layouts  1.09 us (2%)
    pallas_call x1, Pallas kernels, team_scores(): pl.pallas_call(team_kernel, out_shape=jax.ShapeDtypeStruct((1, rows), f32...  55.2 us

profile of v1, /device:TPU:0, one launch (start us, length us, event | category | flops | bytes accessed | tf_op | source)
XLA Modules:
  0.0 70.6 jit_solution(13660242985856880396)
XLA Ops:
  6.5 55.2 %team_scores.1 = f32[1,512]{1,0:T(1,128)S(1)} custom-call(bf16[512,768]{1,0:T(8,128)(2,1)} %embed_ref.1, s32[1,512]{1,0:T(1,128)} %bitcast.56, s32[1,512]{1,0:T(1,128)} %bitcast.61), custom_call_target="tpu_custom_call" | custom-call | tf_op jit(solution)/shard_map/team_scores/pallas_call | solution.py:410
  61.8 0.5 slice.9
  62.9 0.2 conditional.2
  63.2 0.6 copy.31

commit v2 on v0

v2 whole, which is shorter than its diff:
```python
import functools
import types

import jax
import jax.numpy as jnp
from jax import lax
from jax.experimental import pallas as pl
from jax.experimental.pallas import tpu as pltpu
from jax.sharding import PartitionSpec as P

MESH = pl.DeviceIdType.MESH
SIDE = 4
CELLS = 64
CELL = 16
SPILL = 80
LANES = 128
QUARTER = 256
SLOTS = CELLS * CELL
FORWARD = 3 * SPILL
LEFT_SPILL = 256
NONE = -4.0
FAILED = 8.0
EMPTY = 2.0


def split3(value):
    high = value.astype(jnp.bfloat16)
    rest = value - high.astype(jnp.float32)
    mid = rest.astype(jnp.bfloat16)
    low = (rest - mid.astype(jnp.float32)).astype(jnp.bfloat16)
    return high, mid, low


def iota(shape, dim):
    return lax.broadcasted_iota(jnp.int32, shape, dim)


def dot(left, right):
    return jnp.dot(left, right, preferred_element_type=jnp.float32)


def dot_t(left, right):
    return lax.dot_general(left, right, (((1,), (1,)), ((), ())), preferred_element_type=jnp.float32)


def fold(scores):
    rows, columns = scores.shape
    return jnp.max(scores.reshape(rows // 8, 8, columns), axis=0)


def column(tags, index):
    return jnp.transpose(tags)[:, index : index + 1]


class Place:
    def __init__(self):
        group = lax.axis_index("group")
        member = lax.axis_index("member")
        self.y, self.z = group // SIDE, group % SIDE
        self.x, self.core = member // 2, member % 2
        self.cell = group * SIDE + self.x
        self.sum = (self.y + self.z + self.x) % SIDE
        self.source = self.sum * 16 + self.y * SIDE + self.z
        self.sibling = self.at(0, 0, 0, 1)[2]

    def at(self, dy, dz, dx, dcore=0):
        y, z, x = (self.y + dy) % SIDE, (self.z + dz) % SIDE, (self.x + dx) % SIDE
        plane = y * SIDE + z
        source = ((y + z + x) % SIDE) * 16 + plane
        device = {"group": plane, "member": x * 2 + (self.core + dcore) % 2}
        return plane * SIDE + x, source, device

    def offset(self, phase, index):
        dy, dz = index // SIDE, index % SIDE
        return self.at(dy, dz, (phase + 8 - dy - dz) % SIDE)


def wait_for(ref, sem):
    pltpu.make_async_copy(ref, ref, sem).wait()


def greet(place, s):
    barrier = pltpu.get_barrier_semaphore()
    for d in range(1, SIDE):
        for offset in ((d, 0, 0), (0, d, 0), (0, 0, d)):
            device = place.at(*offset)[2]
            pl.semaphore_signal(barrier, inc=1, device_id=device, device_id_type=MESH)
    pl.semaphore_signal(barrier, inc=1, device_id=place.sibling, device_id_type=MESH)
    return barrier


def regroup(place, s):
    load = [
        pltpu.make_async_copy(src, dst, s.load_sems.at[n])
        for n, (src, dst) in enumerate(
            ((s.dest_hbm, s.dest), (s.cluster_hbm, s.cluster), (s.embed_hbm, s.embed))
        )
    ]
    for copy in load:
        copy.start()
    barrier = greet(place, s)
    load[0].wait()
    load[1].wait()

    rows = s.dest.shape[1]
    team = lax.shift_right_logical(s.dest[...], 3)
    cluster = s.cluster[...]
    in_team = (iota((16, rows), 0) == team).astype(jnp.float32)
    cells = jnp.concatenate(
        [in_team * (cluster == c).astype(jnp.float32) for c in range(4)], axis=0
    )
    earlier = (iota((rows, rows), 0) < iota((rows, rows), 1)).astype(jnp.bfloat16)
    rank = jnp.sum(cells * dot(cells.astype(jnp.bfloat16), earlier), axis=0, keepdims=True)
    counts = jnp.minimum(jnp.sum(cells, axis=1, keepdims=True), float(CELL))
    over = rank >= float(CELL)
    over_team = in_team * over.astype(jnp.float32)
    order = jnp.sum(
        over_team * dot(over_team.astype(jnp.bfloat16), earlier), axis=0, keepdims=True
    )
    filled = [
        jnp.sum(in_team * counts[16 * c : 16 * c + 16], axis=0, keepdims=True) for c in range(4)
    ]
    free0 = CELL - filled[0]
    free1 = free0 + CELL - filled[1]
    free2 = free1 + CELL - filled[2]
    chip = (
        (order >= free0).astype(jnp.int32)
        + (order >= free1).astype(jnp.int32)
        + (order >= free2).astype(jnp.int32)
    )
    spot = jnp.where(
        chip == 0,
        filled[0] + order,
        jnp.where(
            chip == 1,
            filled[1] + order - free0,
            jnp.where(chip == 2, filled[2] + order - free1, filled[3] + order - free2),
        ),
    )
    chip = jnp.where(over, chip, cluster)
    spot = jnp.where(over, spot, rank).astype(jnp.int32)
    cell = team * 4 + chip
    dy = lax.rem(lax.shift_right_logical(team, 2) + (SIDE - place.y), SIDE)
    dz = lax.rem(lax.rem(team, SIDE) + (SIDE - place.z), SIDE)
    dx = lax.rem(chip + (SIDE - place.x), SIDE)
    slot = lax.rem(dy + dz + dx, SIDE) * QUARTER + (dy * SIDE + dz) * CELL + spot
    lane = spot + (place.source % 8) * CELL

    pl.semaphore_wait(barrier, 10)
    for d in range(1, SIDE):
        device = place.at(0, d, 0)[2]
        pl.semaphore_signal(s.line_sem, inc=1, device_id=device, device_id_type=MESH)

    load[2].wait()
    values = s.embed[...].astype(jnp.float32)
    norm = jnp.sum(values * values, axis=1, keepdims=True)
    s.unit[...] = (values * lax.rsqrt(norm + 1e-06)).astype(jnp.bfloat16)

    pl.semaphore_wait(s.line_sem, 3)
    for d in range(1, SIDE):
        device = place.at(0, 0, d)[2]
        pl.semaphore_signal(s.plane_sem, inc=1, device_id=device, device_id_type=MESH)

    in_cell = (iota((CELLS, rows), 0) == cell).astype(jnp.float32)
    at_lane = (iota((LANES, rows), 0) == lane).astype(jnp.bfloat16)
    labels = (in_cell * (cluster + 1).astype(jnp.float32)).astype(jnp.bfloat16)
    s.meta[...] = dot_t(labels, at_lane).reshape(CELLS, 1, LANES)

    send, left = s.send, s.left

    def landing(index):
        return pl.ds(pl.multiple_of(index * CELL, CELL), CELL)

    for phase in range(SIDE):
        base = phase * QUARTER
        chosen = (iota((QUARTER, rows), 0) + base == slot).astype(jnp.bfloat16)
        send[base : base + QUARTER] = dot(chosen, s.unit[...]).astype(jnp.bfloat16)
        if phase == 0:
            pl.semaphore_wait(s.plane_sem, 3)
            pltpu.make_async_copy(
                send.at[pl.ds(0, CELL)], left.at[landing(place.source)], s.recv_sems.at[0]
            ).start()
            pltpu.make_async_copy(
                s.meta.at[pl.ds(place.cell, 1)],
                s.meta_in.at[pl.ds(place.source, 1)],
                s.meta_sem,
            ).start()

        def send_cell(index, carry, phase=phase, base=base):
            target, _, device = place.offset(phase, index)
            pltpu.make_async_remote_copy(
                src_ref=send.at[landing(phase * 16 + index)],
                dst_ref=left.at[landing(place.source)],
                send_sem=s.send_sems.at[0],
                recv_sem=s.recv_sems.at[phase],
                device_id=device,
                device_id_type=MESH,
            ).start()
            pltpu.make_async_remote_copy(
                src_ref=s.meta.at[pl.ds(target, 1)],
                dst_ref=s.meta_in.at[pl.ds(place.source, 1)],
                send_sem=s.send_sems.at[1],
                recv_sem=s.meta_sem,
                device_id=device,
                device_id_type=MESH,
            ).start()
            return carry

        lax.fori_loop(1 if phase == 0 else 0, 16, send_cell, 0)
    return in_cell, at_lane, team, cluster, chip


def arrived(place, phase):
    base = ((place.sum + SIDE - phase) % SIDE) * QUARTER
    return pl.ds(pl.multiple_of(base, QUARTER), QUARTER)


def to_sources(place, source_ref, dest_ref, send_sem, recv_sem):
    def send_one(index, carry):
        _, source, device = place.offset(index // 16, index % 16)
        pltpu.make_async_remote_copy(
            src_ref=source_ref.at[pl.ds(source // 8, 1)],
            dst_ref=dest_ref.at[pl.ds(place.cell, 1)],
            send_sem=send_sem,
            recv_sem=recv_sem,
            device_id=device,
            device_id_type=MESH,
        ).start()
        return carry

    lax.fori_loop(1, CELLS, send_one, 0)
    pltpu.make_async_copy(
        source_ref.at[pl.ds(place.source // 8, 1)], dest_ref.at[pl.ds(place.cell, 1)], recv_sem
    ).start()


def wait_sent(s):
    sent = pl.ds(0, SLOTS - CELL)
    wait_for(s.send.at[sent], s.send_sems.at[0])
    sent = pl.ds(0, CELLS - 1)
    wait_for(s.meta.at[sent], s.send_sems.at[1])


def team_kernel(names, *refs):
    s = types.SimpleNamespace(**dict(zip(names, refs)))
    place = Place()
    in_cell, at_lane, team, cluster, chip = regroup(place, s)
    left, other = s.left, s.other
    left[SLOTS + FORWARD :] = jnp.zeros((LEFT_SPILL - FORWARD, left.shape[1]), jnp.bfloat16)

    def to_pair(src, dst, index):
        copy = pltpu.make_async_remote_copy(
            src_ref=src,
            dst_ref=dst,
            send_sem=s.pair_sems.at[0, index],
            recv_sem=s.pair_sems.at[1, index],
            device_id=place.sibling,
            device_id_type=MESH,
        )
        copy.start()
        return copy

    shared = []
    for phase in range(SIDE):
        part = arrived(place, phase)
        wait_for(left.at[part], s.recv_sems.at[phase])
        shared.append(to_pair(left.at[part], other.at[part], phase))
    wait_for(s.meta_in, s.meta_sem)

    label = jnp.sum(s.meta_in[...].reshape(8, 8, LANES), axis=1)
    own = (place.x + 1).astype(jnp.float32)
    below = (iota((LANES, LANES), 0) < iota((LANES, LANES), 1)).astype(jnp.bfloat16)
    hits = [
        (label == (lax.rem(place.x + d, SIDE) + 1).astype(jnp.float32)).astype(jnp.float32)
        for d in range(1, SIDE)
    ]
    hit = jnp.concatenate(hits, axis=0)
    within = dot(hit.astype(jnp.bfloat16), below)
    totals = jnp.sum(hit, axis=1, keepdims=True)
    places = jnp.full((8, LANES), -1.0, jnp.float32)
    worst = jnp.zeros((1, 1), jnp.float32)
    row, col = iota((8, 8), 0), iota((8, 8), 1)
    for d in range(3):
        total = totals[8 * d : 8 * d + 8]
        spread = jnp.broadcast_to(total, (8, 8))
        before = jnp.sum(jnp.where(row < col, spread, 0.0), axis=0, keepdims=True)
        spread = jnp.broadcast_to(before, (8, 8))
        before = jnp.sum(jnp.where(row == col, spread, 0.0), axis=1, keepdims=True)
        position = within[8 * d : 8 * d + 8] + before
        places = jnp.where(
            (hits[d] > 0.0) & (position < float(SPILL)), position + float(SPILL * d), places
        )
        worst = jnp.maximum(worst, jnp.sum(total, axis=0, keepdims=True))
    failed = jnp.broadcast_to((worst > float(SPILL)).astype(jnp.float32), (8, LANES))
    select, forward = s.select, s.forward
    for q in range(8):
        select[:, q * LANES : (q + 1) * LANES] = (
            iota((FORWARD, LANES), 0).astype(jnp.float32) == places[q : q + 1]
        ).astype(jnp.bfloat16)
    chosen = select[...]
    taken = jnp.sum(chosen.astype(jnp.float32), axis=1, keepdims=True)
    moved = dot(chosen, left[0:SLOTS])
    mark = jnp.where((iota((FORWARD, LANES), 1) == 0) & (taken < 0.5), EMPTY, 0.0)
    forward[:, 0:LANES] = (moved[:, 0:LANES] + mark).astype(jnp.bfloat16)
    forward[:, LANES:] = moved[:, LANES:].astype(jnp.bfloat16)
    to_line = []
    for d in range(3):
        copy = pltpu.make_async_remote_copy(
            src_ref=forward.at[pl.ds(d * SPILL, SPILL)],
            dst_ref=left.at[pl.ds(SLOTS + d * SPILL, SPILL)],
            send_sem=s.spill_sems.at[0, d],
            recv_sem=s.spill_sems.at[1, d],
            device_id=place.at(0, 0, d + 1)[2],
            device_id_type=MESH,
        )
        copy.start()
        to_line.append(copy)
    s.label_out[0:8] = label
    s.label_out[8:16] = failed
    copy_label = to_pair(s.label_out, s.label_in, 4)
    s.places_out[...] = places.reshape(8, 1, LANES)
    to_sources(place, s.places_out, s.places_in, s.send_sems.at[2], s.places_sem)

    def set_bias(ref, tags):
        for q in range(8):
            ref[q * LANES : (q + 1) * LANES, 0:1] = jnp.where(column(tags, q) == own, 0.0, NONE)

    def against(right, right_bias, first, count, same):
        def one(index, best):
            base = pl.multiple_of(index * QUARTER, QUARTER)
            part = pl.ds(base, QUARTER)
            scores = dot_t(right[part], left[first : first + count]) + right_bias[part, 0:1]
            if same:
                scores = jnp.where(
                    iota((QUARTER, count), 0) + base == iota((QUARTER, count), 1), NONE, scores
                )
            return jnp.maximum(best, fold(scores))

        start = jnp.full((8, count), NONE, jnp.float32)
        return lax.fori_loop(0, SLOTS // QUARTER, one, start)

    bias, other_bias = s.bias, s.other_bias
    set_bias(bias, label)
    best_main = against(left, bias, 0, SLOTS, True)
    copy_label.wait()
    set_bias(other_bias, s.label_in[0:8])
    for copy in shared:
        copy.wait()
    best_main = jnp.maximum(best_main, against(other, other_bias, 0, SLOTS, False))

    for copy in to_line:
        copy.wait()
    spill_pair = to_pair(left.at[pl.ds(SLOTS, FORWARD)], s.other_spill, 5)
    best_spill = against(left, bias, SLOTS, LEFT_SPILL, False)
    best_spill = jnp.maximum(best_spill, against(other, other_bias, SLOTS, LEFT_SPILL, False))

    def against_spill(right, same):
        scores = dot_t(right, left[...]) + jnp.where(
            right[:, 0:1].astype(jnp.float32) > 1.5, NONE, 0.0
        )
        if same:
            scores = jnp.where(
                iota(scores.shape, 0) + SLOTS == iota(scores.shape, 1), NONE, scores
            )
        return fold(scores)

    best_all = against_spill(left[SLOTS : SLOTS + FORWARD], True)
    rows = cluster.shape[1]
    wait_for(s.places_in, s.places_sem)
    held = dot(s.places_in[...].reshape(CELLS, LANES).astype(jnp.bfloat16), at_lane)
    held = jnp.sum(held * in_cell, axis=0, keepdims=True).astype(jnp.int32)
    at_held = (iota((LEFT_SPILL, rows), 0) == held).astype(jnp.bfloat16)
    in_own = (iota((CELLS, rows), 0) == team * 4 + cluster).astype(jnp.float32)
    spill_pair.wait()
    best_all = jnp.maximum(best_all, against_spill(s.other_spill[...], False))
    best_main = jnp.max(jnp.maximum(best_main, best_all[:, 0:SLOTS]), axis=0, keepdims=True)
    best_spill = jnp.max(jnp.maximum(best_spill, best_all[:, SLOTS:]), axis=0, keepdims=True)

    failed = jnp.maximum(failed, s.label_in[8:16])[0:1]
    best_out = s.best_out
    for q in range(8):
        part = best_main[:, q * LANES : (q + 1) * LANES]
        best_out[q, :, 0:LANES] = jnp.where(failed > 0.0, FAILED, part)
        best_out[q, :, LANES:] = best_spill
    to_sources(place, best_out, s.best_in, s.send_sems.at[3], s.best_sem)
    wait_for(s.best_in, s.best_sem)
    found = s.best_in[...].reshape(CELLS, LANES + LEFT_SPILL)
    worst = jnp.max(jnp.max(found, axis=1, keepdims=True), axis=0, keepdims=True)
    straight = sum(dot(piece, at_lane) for piece in split3(found[:, 0:LANES]))
    straight = jnp.sum(straight * in_cell, axis=0, keepdims=True)
    moved = sum(dot(piece, at_held) for piece in split3(found[:, LANES:]))
    moved = jnp.sum(moved * in_own, axis=0, keepdims=True)
    score = jnp.maximum(jnp.where(chip == cluster, straight, moved), -1.0)
    s.out[...] = jnp.where(worst > 4.0, FAILED, score)

    wait_sent(s)
    sent = pl.ds(0, CELLS - 1)
    wait_for(s.places_in.at[sent], s.send_sems.at[2])
    wait_for(s.best_in.at[sent], s.send_sems.at[3])


def general_kernel(names, *refs):
    s = types.SimpleNamespace(**dict(zip(names, refs)))
    place = Place()
    in_cell, at_lane, _, _, _ = regroup(place, s)
    left = s.left
    for phase in range(SIDE):
        wait_for(left.at[arrived(place, phase)], s.recv_sems.at[phase])
    wait_for(s.meta_in, s.meta_sem)
    label = jnp.sum(s.meta_in[...].reshape(8, 8, LANES), axis=1)
    s.label_out[...] = label
    copies = []
    for block in range(1, 8):
        for index, (src, dst) in enumerate(((left, s.gather), (s.label_out, s.tags))):
            copy = pltpu.make_async_remote_copy(
                src_ref=src,
                dst_ref=dst.at[block - 1],
                send_sem=s.line_sems.at[0, index, block - 1],
                recv_sem=s.line_sems.at[1, index, block - 1],
                device_id=place.at(0, 0, block // 2, block % 2)[2],
                device_id_type=MESH,
            )
            copy.start()
            copies.append(copy)
    left_label = jnp.concatenate([label[q : q + 1] for q in range(8)], axis=1)

    def against(right, tags, same):
        for q in range(8):
            s.bias[q * LANES : (q + 1) * LANES, 0:1] = column(tags, q)

        def one(index, best):
            base = pl.multiple_of(index * QUARTER, QUARTER)
            part = pl.ds(base, QUARTER)
            scores = dot_t(right[part], left[...])
            counts = s.bias[part, 0:1] == left_label
            if same:
                shape = (QUARTER, SLOTS)
                counts = counts & (iota(shape, 0) + base != iota(shape, 1))
            return jnp.maximum(best, fold(jnp.where(counts, scores, NONE)))

        start = jnp.full((8, SLOTS), NONE, jnp.float32)
        return lax.fori_loop(0, SLOTS // QUARTER, one, start)

    best = against(left, label, True)
    for copy in copies:
        copy.wait()

    def block(index, best):
        return jnp.maximum(best, against(s.gather.at[index], s.tags[index], False))

    best = jnp.max(lax.fori_loop(0, 7, block, best), axis=0, keepdims=True)
    for q in range(8):
        s.best_out[q] = best[:, q * LANES : (q + 1) * LANES]
    to_sources(place, s.best_out, s.best_in, s.send_sems.at[2], s.best_sem)
    wait_for(s.best_in, s.best_sem)
    found = s.best_in[...].reshape(CELLS, LANES)
    score = sum(dot(piece, at_lane) for piece in split3(found))
    s.out[...] = jnp.maximum(jnp.sum(score * in_cell, axis=0, keepdims=True), -1.0)
    wait_sent(s)
    wait_for(s.best_in.at[pl.ds(0, CELLS - 1)], s.send_sems.at[2])


def call(kernel, name, collective, extra, embed, destination, cluster):
    rows, features = embed.shape
    bf16, f32, i32 = jnp.bfloat16, jnp.float32, jnp.int32
    vmem, dma = pltpu.VMEM, pltpu.SemaphoreType.DMA
    scratch = dict(
        dest=vmem((1, rows), i32),
        cluster=vmem((1, rows), i32),
        embed=vmem((rows, features), bf16),
        unit=vmem((rows, features), bf16),
        send=vmem((SLOTS, features), bf16),
        meta=vmem((CELLS, 1, LANES), f32),
        meta_in=vmem((CELLS, 1, LANES), f32),
        bias=vmem((SLOTS, LANES), f32),
        line_sem=pltpu.SemaphoreType.REGULAR,
        plane_sem=pltpu.SemaphoreType.REGULAR,
        load_sems=dma((3,)),
        send_sems=dma((4,)),
        recv_sems=dma((SIDE,)),
        meta_sem=dma,
        best_sem=dma,
        **extra(features),
    )
    names = ("dest_hbm", "cluster_hbm", "embed_hbm", "out", *scratch)
    return pl.pallas_call(
        functools.partial(kernel, names),
        out_shape=jax.ShapeDtypeStruct((1, rows), f32),
        in_specs=[pl.BlockSpec(memory_space=pl.ANY)] * 3,
        out_specs=pl.BlockSpec(memory_space=pltpu.VMEM),
        scratch_shapes=list(scratch.values()),
        compiler_params=pltpu.CompilerParams(
            collective_id=collective, has_side_effects=True, vmem_limit_bytes=40 * 2**20
        ),
        name=name,
    )(destination.reshape(1, rows), cluster.reshape(1, rows), embed)


def team_scratch(features):
    bf16, f32, vmem, dma = jnp.bfloat16, jnp.float32, pltpu.VMEM, pltpu.SemaphoreType.DMA
    return dict(
        left=vmem((SLOTS + LEFT_SPILL, features), bf16),
        other=vmem((SLOTS, features), bf16),
        other_spill=vmem((FORWARD, features), bf16),
        select=vmem((FORWARD, SLOTS), bf16),
        forward=vmem((FORWARD, features), bf16),
        label_out=vmem((16, LANES), f32),
        label_in=vmem((16, LANES), f32),
        other_bias=vmem((SLOTS, LANES), f32),
        places_out=vmem((8, 1, LANES), f32),
        places_in=vmem((CELLS, 1, LANES), f32),
        best_out=vmem((8, 1, LANES + LEFT_SPILL), f32),
        best_in=vmem((CELLS, 1, LANES + LEFT_SPILL), f32),
        places_sem=dma,
        pair_sems=dma((2, 6)),
        spill_sems=dma((2, 3)),
    )


def general_scratch(features):
    bf16, f32, vmem, dma = jnp.bfloat16, jnp.float32, pltpu.VMEM, pltpu.SemaphoreType.DMA
    return dict(
        left=vmem((SLOTS, features), bf16),
        gather=vmem((7, SLOTS, features), bf16),
        label_out=vmem((8, LANES), f32),
        tags=vmem((7, 8, LANES), f32),
        best_out=vmem((8, 1, LANES), f32),
        best_in=vmem((CELLS, 1, LANES), f32),
        line_sems=dma((2, 2, 7)),
    )


def shards(embed, destination, cluster):
    rows = embed.shape[0]
    scores = call(team_kernel, "team_scores", 0, team_scratch, embed, destination, cluster)

    def general(*args):
        return call(general_kernel, "general_scores", 1, general_scratch, *args).reshape(rows)

    return lax.cond(
        scores[0, 0] > 4.0,
        general,
        lambda *unused: scores.reshape(rows),
        embed,
        destination,
        cluster,
    )


def solution(mesh):
    in_specs = (P(("group", "member"), None), P(("group", "member")), P(("group", "member")))
    out_specs = P(("group", "member"))
    return jax.shard_map(shards, mesh=mesh, in_specs=in_specs, out_specs=out_specs, check_vma=False)
```

time: 362 us -> 55.4 us (0.15)
  loops' own time: 86.8 us -> 0.01 us
  local copies, waits for them, and re-layouts: 67.6 us -> 1.1 us
  waiting for transfers between devices: 66.3 us -> 0 us
  matrix products: 56 us -> 0 us
  Pallas kernels: 0 us -> 53.5 us
  starting transfers between devices: 28.8 us -> 0 us
  blocking collectives: 25.7 us -> 0 us
  other arithmetic: 13.6 us -> 0 us
  between operations: 13.6 us -> 0.71 us
    another operation x35 -> x1, loops' own time: 86.8 us -> 0.01 us  [shards(): lax.cond(scores[0, 0] > 4.0, general, lambda *unused: scores.reshape(rows...]
    dot_general x30 -> x0, matrix products: 56 us -> none  [compute(): lax.dot_general(piece_rows, tile_rows, (((1,), (1,)), ((), ())), preferre...]
    pallas_call x0 -> x1, Pallas kernels: none -> 53.5 us  [call(): pl.pallas_call(functools.partial(kernel, names), out_shape=jax.ShapeDtype...]
    dynamic_slice x100 -> x0, local copies, waits for them, and re-layouts: 43.9 us -> none  [the longest x94 42.1 us: one_block(): lax.scan(one_column, jnp.full((block_size,), -2.0, jnp.float32), (right_t...]
    all_to_all x3 -> x0, waiting for transfers between devices: 33.3 us -> none  [the longest x1 18.9 us: shards(): lax.all_to_all(outgoing.reshape(devices, per_pair, feature_dim), ('group'...]
    all_gather x1 -> x0, waiting for transfers between devices: 33 us -> none  [shards(): lax.all_gather(own_block, 'member', axis=0, tiled=True)]
    all_to_all x3 -> x0, starting transfers between devices: 28.8 us -> none  [the longest x1 12.8 us: shards(): lax.all_to_all(scores.reshape(devices, per_pair), ('group', 'member'), sp...]
    all_gather x2 -> x0, blocking collectives: 25.7 us -> none  [the longest x1 12.8 us: shards(): lax.all_gather(own_labels, 'member', axis=0, tiled=True)]
  transfers between devices with their start and end apart: 4 -> 0, of which waited for: 4 -> 0; matrix products, arithmetic and copies ran while one was open for 4% -> 0% of each run, Pallas kernels for 0% -> 0%
where the time goes in v2:
time: 55.4 us; the launch traced here: 55.3 us
  Pallas kernels  53.5 us (97%)
  local copies, waits for them, and re-layouts  1.1 us (2%)
  between operations  0.71 us (1%)
    pallas_call x1, Pallas kernels, call(): pl.pallas_call(functools.partial(kernel, names), out_shape=jax.ShapeDtype...  53.5 us

profile of v2, /device:TPU:0, one launch (start us, length us, event | category | flops | bytes accessed | tf_op | source)
XLA Modules:
  0.0 55.3 jit_solution(17801867074709330203)
XLA Ops:
  0.0 0.0 copy-start
  0.0 0.0 copy-start.2
  0.0 53.5 %team_scores.1 = f32[1,512]{1,0:T(1,128)S(1)} custom-call(s32[1,512]{1,0:T(1,128)} %bitcast.7, s32[1,512]{1,0:T(1,128)} %bitcast.9, bf16[512,768]{1,0:T(8,128)(2,1)} %refs_2_.1), custom_call_target="tpu_custom_call" | custom-call | tf_op jit(solution)/shard_map/team_scores/pallas_call | solution.py:486
  53.5 0.5 slice.3
  54.0 0.0 copy-start.1
  54.7 0.0 copy-done
  54.7 0.0 copy-done.2
  54.7 0.0 copy-done.1
  54.7 0.6 %copy.10 = f32[512]{0:T(512)} copy(f32[512]{0:T(512)S(1)} %get-tuple-element.18) | data formatting | bytes 4096
  (1 shorter events, 0.0 us)
Async XLA Ops:
  0.0 54.7 %copy-start = (bf16[512,768]{1,0:T(8,128)(2,1)S(1)}, bf16[512,768]{1,0:T(8,128)(2,1)}, u32[]{:S(2)}) copy-start(bf16[512,768]{1,0:T(8,128)(2,1)} %refs_2_.1) | copy-start | bytes 2359300
  0.0 54.7 %copy-start.2 = (s32[512]{0:T(512)S(1)}, s32[512]{0:T(512)}, u32[]{:S(2)}) copy-start(s32[512]{0:T(512)} %param.7) | copy-start | bytes 6148
  54.0 0.7 %copy-start.1 = (s32[512]{0:T(512)S(1)}, s32[512]{0:T(512)}, u32[]{:S(2)}) copy-start(s32[512]{0:T(512)} %param.6) | copy-start | bytes 6148

commit v3 on v2

--- a/solution.py
+++ b/solution.py
@@ -19,6 +19,8 @@
 FORWARD = 3 * SPILL
 LEFT_SPILL = 256
 NONE = -4.0
+META_AFTER = 0
+ENTRY = 3
 FAILED = 8.0
 EMPTY = 2.0
 
@@ -56,23 +58,34 @@
     def __init__(self):
         group = lax.axis_index("group")
         member = lax.axis_index("member")
-        self.y, self.z = group // SIDE, group % SIDE
-        self.x, self.core = member // 2, member % 2
-        self.cell = group * SIDE + self.x
-        self.sum = (self.y + self.z + self.x) % SIDE
-        self.source = self.sum * 16 + self.y * SIDE + self.z
-        self.sibling = self.at(0, 0, 0, 1)[2]
-
-    def at(self, dy, dz, dx, dcore=0):
-        y, z, x = (self.y + dy) % SIDE, (self.z + dz) % SIDE, (self.x + dx) % SIDE
-        plane = y * SIDE + z
-        source = ((y + z + x) % SIDE) * 16 + plane
-        device = {"group": plane, "member": x * 2 + (self.core + dcore) % 2}
-        return plane * SIDE + x, source, device
-
-    def offset(self, phase, index):
-        dy, dz = index // SIDE, index % SIDE
-        return self.at(dy, dz, (phase + 8 - dy - dz) % SIDE)
+        y, z = group // SIDE, group % SIDE
+        x, self.core = member // 2, member % 2
+        self.ys = [y] + [(y + d) % SIDE for d in range(1, SIDE)]
+        self.zs = [z] + [(z + d) % SIDE for d in range(1, SIDE)]
+        self.xs = [x] + [(x + d) % SIDE for d in range(1, SIDE)]
+        self.y, self.z, self.x = y, z, x
+        self.cell = group * SIDE + x
+        self.sum = (y + z + x) % SIDE
+        self.sums = [self.sum] + [(self.sum + d) % SIDE for d in range(1, SIDE)]
+        self.source = self.sum * 16 + group
+        self.halves = [value // 2 for value in self.ys]
+        self.sibling = {"group": group, "member": x * 2 + 1 - self.core}
+
+    def at(self, dy, dz, dx):
+        return {"group": self.ys[dy] * SIDE + self.zs[dz], "member": self.xs[dx] * 2 + self.core}
+
+    def cell_at(self, dy, dz, dx):
+        return (self.ys[dy] * SIDE + self.zs[dz]) * SIDE + self.xs[dx]
+
+    def eight_at(self, dy, dz, dx):
+        return self.sums[(dy + dz + dx) % SIDE] * 2 + self.halves[dy]
+
+
+def offsets(phase):
+    return [(dy, dz, (phase - dy - dz) % SIDE) for dy in range(SIDE) for dz in range(SIDE)]
+
+
+OTHERS = [offset for phase in range(SIDE) for offset in offsets(phase)][1:]
 
 
 def wait_for(ref, sem):
@@ -83,7 +96,7 @@
     barrier = pltpu.get_barrier_semaphore()
     for d in range(1, SIDE):
         for offset in ((d, 0, 0), (0, d, 0), (0, 0, d)):
-            device = place.at(*offset)[2]
+            device = place.at(*offset)
             pl.semaphore_signal(barrier, inc=1, device_id=device, device_id_type=MESH)
     pl.semaphore_signal(barrier, inc=1, device_id=place.sibling, device_id_type=MESH)
     return barrier
@@ -148,7 +161,7 @@
 
     pl.semaphore_wait(barrier, 10)
     for d in range(1, SIDE):
-        device = place.at(0, d, 0)[2]
+        device = place.at(0, d, 0)
         pl.semaphore_signal(s.line_sem, inc=1, device_id=device, device_id_type=MESH)
 
     load[2].wait()
@@ -158,7 +171,7 @@
 
     pl.semaphore_wait(s.line_sem, 3)
     for d in range(1, SIDE):
-        device = place.at(0, 0, d)[2]
+        device = place.at(0, 0, d)
         pl.semaphore_signal(s.plane_sem, inc=1, device_id=device, device_id_type=MESH)
 
     in_cell = (iota((CELLS, rows), 0) == cell).astype(jnp.float32)
@@ -180,57 +193,65 @@
             pltpu.make_async_copy(
                 send.at[pl.ds(0, CELL)], left.at[landing(place.source)], s.recv_sems.at[0]
             ).start()
-            pltpu.make_async_copy(
-                s.meta.at[pl.ds(place.cell, 1)],
-                s.meta_in.at[pl.ds(place.source, 1)],
-                s.meta_sem,
-            ).start()
-
-        def send_cell(index, carry, phase=phase, base=base):
-            target, _, device = place.offset(phase, index)
-            pltpu.make_async_remote_copy(
-                src_ref=send.at[landing(phase * 16 + index)],
-                dst_ref=left.at[landing(place.source)],
-                send_sem=s.send_sems.at[0],
-                recv_sem=s.recv_sems.at[phase],
-                device_id=device,
-                device_id_type=MESH,
-            ).start()
-            pltpu.make_async_remote_copy(
-                src_ref=s.meta.at[pl.ds(target, 1)],
-                dst_ref=s.meta_in.at[pl.ds(place.source, 1)],
-                send_sem=s.send_sems.at[1],
-                recv_sem=s.meta_sem,
-                device_id=device,
-                device_id_type=MESH,
-            ).start()
-            return carry
-
-        lax.fori_loop(1 if phase == 0 else 0, 16, send_cell, 0)
-    return in_cell, at_lane, team, cluster, chip
+
+        for index, offset in enumerate(offsets(phase)):
+            if any(offset):
+                pltpu.make_async_remote_copy(
+                    src_ref=send.at[landing(phase * 16 + index)],
+                    dst_ref=left.at[landing(place.source)],
+                    send_sem=s.send_sems.at[0],
+                    recv_sem=s.recv_sems.at[phase],
+                    device_id=place.at(*offset),
+                    device_id_type=MESH,
+                ).start()
+        if phase == META_AFTER:
+            send_labels(place, s)
+    return in_cell, at_lane, team, cluster, chip, lane
+
+
+def send_labels(place, s):
+    for offset in OTHERS:
+        pltpu.make_async_remote_copy(
+            src_ref=s.meta.at[pl.ds(place.cell_at(*offset), 1)],
+            dst_ref=s.meta_in.at[pl.ds(place.source, 1)],
+            send_sem=s.send_sems.at[1],
+            recv_sem=s.meta_sem,
+            device_id=place.at(*offset),
+            device_id_type=MESH,
+        ).start()
+    pltpu.make_async_copy(
+        s.meta.at[pl.ds(place.cell, 1)], s.meta_in.at[pl.ds(place.source, 1)], s.meta_sem
+    ).start()
+
+
+def quarter(place, phase):
+    if isinstance(phase, int):
+        return place.sums[-phase % SIDE]
+    return (place.sum + SIDE - phase) % SIDE
+
+
+def rows_of(index):
+    return pl.ds(pl.multiple_of(index * QUARTER, QUARTER), QUARTER)
 
 
 def arrived(place, phase):
-    base = ((place.sum + SIDE - phase) % SIDE) * QUARTER
-    return pl.ds(pl.multiple_of(base, QUARTER), QUARTER)
-
-
-def to_sources(place, source_ref, dest_ref, send_sem, recv_sem):
-    def send_one(index, carry):
-        _, source, device = place.offset(index // 16, index % 16)
+    return rows_of(quarter(place, phase))
+
+
+def to_sources(place, source_ref, dest_ref, size, send_sem, recv_sem):
+    for offset in OTHERS:
         pltpu.make_async_remote_copy(
-            src_ref=source_ref.at[pl.ds(source // 8, 1)],
-            dst_ref=dest_ref.at[pl.ds(place.cell, 1)],
+            src_ref=source_ref.at[pl.ds(place.eight_at(*offset) * size, size)],
+            dst_ref=dest_ref.at[pl.ds(place.cell * size, size)],
             send_sem=send_sem,
             recv_sem=recv_sem,
-            device_id=device,
+            device_id=place.at(*offset),
             device_id_type=MESH,
         ).start()
-        return carry
-
-    lax.fori_loop(1, CELLS, send_one, 0)
     pltpu.make_async_copy(
-        source_ref.at[pl.ds(place.source // 8, 1)], dest_ref.at[pl.ds(place.cell, 1)], recv_sem
+        source_ref.at[pl.ds(place.source // 8 * size, size)],
+        dest_ref.at[pl.ds(place.cell * size, size)],
+        recv_sem,
     ).start()
 
 
@@ -244,7 +265,7 @@
 def team_kernel(names, *refs):
     s = types.SimpleNamespace(**dict(zip(names, refs)))
     place = Place()
-    in_cell, at_lane, team, cluster, chip = regroup(place, s)
+    in_cell, at_lane, team, cluster, chip, lane = regroup(place, s)
     left, other = s.left, s.other
     left[SLOTS + FORWARD :] = jnp.zeros((LEFT_SPILL - FORWARD, left.shape[1]), jnp.bfloat16)
 
@@ -260,13 +281,7 @@
         copy.start()
         return copy
 
-    shared = []
-    for phase in range(SIDE):
-        part = arrived(place, phase)
-        wait_for(left.at[part], s.recv_sems.at[phase])
-        shared.append(to_pair(left.at[part], other.at[part], phase))
     wait_for(s.meta_in, s.meta_sem)
-
     label = jnp.sum(s.meta_in[...].reshape(8, 8, LANES), axis=1)
     own = (place.x + 1).astype(jnp.float32)
     below = (iota((LANES, LANES), 0) < iota((LANES, LANES), 1)).astype(jnp.bfloat16)
@@ -292,67 +307,106 @@
         )
         worst = jnp.maximum(worst, jnp.sum(total, axis=0, keepdims=True))
     failed = jnp.broadcast_to((worst > float(SPILL)).astype(jnp.float32), (8, LANES))
+    s.label_out[0:8] = label
+    s.label_out[8:16] = failed
+    copy_label = to_pair(s.label_out, s.label_in, 4)
+    s.places_out[...] = places.reshape(8, 1, LANES)
+    to_sources(place, s.places_out, s.places_in, 1, s.send_sems.at[2], s.places_sem)
     select, forward = s.select, s.forward
     for q in range(8):
-        select[:, q * LANES : (q + 1) * LANES] = (
+        select[q // 2, :, (q % 2) * LANES : (q % 2 + 1) * LANES] = (
             iota((FORWARD, LANES), 0).astype(jnp.float32) == places[q : q + 1]
         ).astype(jnp.bfloat16)
-    chosen = select[...]
-    taken = jnp.sum(chosen.astype(jnp.float32), axis=1, keepdims=True)
-    moved = dot(chosen, left[0:SLOTS])
+    taken = jnp.zeros((FORWARD, 1), jnp.float32)
+    for q in range(SIDE):
+        taken = taken + jnp.sum(select[q].astype(jnp.float32), axis=1, keepdims=True)
     mark = jnp.where((iota((FORWARD, LANES), 1) == 0) & (taken < 0.5), EMPTY, 0.0)
-    forward[:, 0:LANES] = (moved[:, 0:LANES] + mark).astype(jnp.bfloat16)
-    forward[:, LANES:] = moved[:, LANES:].astype(jnp.bfloat16)
+    s.moved[...] = jnp.zeros(s.moved.shape, jnp.float32)
+    s.moved[:, 0:LANES] = mark
+    s.best[...] = jnp.full(s.best.shape, NONE, jnp.float32)
+
+    def set_bias(ref, tags):
+        for q in range(8):
+            ref[q * LANES : (q + 1) * LANES, 0:1] = jnp.where(column(tags, q) == own, 0.0, NONE)
+
+    bias, other_bias = s.bias, s.other_bias
+    set_bias(bias, label)
+    copy_label.wait()
+    set_bias(other_bias, s.label_in[0:8])
+
+    def block(right, right_bias, index, target, same=False):
+        part = rows_of(index)
+        scores = dot_t(right[part], left[rows_of(target)]) + right_bias[part, 0:1]
+        if same:
+            shape = (QUARTER, QUARTER)
+            scores = jnp.where(iota(shape, 0) == iota(shape, 1), NONE, scores)
+        s.best[target] = jnp.maximum(s.best[target], fold(scores))
+
+    def blocks(right, right_bias, phase, same):
+        last = quarter(place, phase)
+        block(right, right_bias, last, last, same)
+
+        def one(index, carry):
+            first = quarter(place, index)
+            block(right, right_bias, last, first)
+            block(right, right_bias, first, last)
+            return carry
+
+        lax.fori_loop(0, phase, one, 0)
+
+    shared = []
+    for phase in range(SIDE):
+        part = arrived(place, phase)
+        wait_for(left.at[part], s.recv_sems.at[phase])
+        shared.append(to_pair(left.at[part], other.at[part], phase))
+        s.moved[...] += dot(select[quarter(place, phase)], left[part])
+        if phase < SIDE - 1:
+            blocks(left, bias, phase, True)
+            if phase > 0:
+                shared[phase - 1].wait()
+                blocks(other, other_bias, phase - 1, False)
+
+    forward[...] = s.moved[...].astype(jnp.bfloat16)
     to_line = []
-    for d in range(3):
+    for d in (1, 0, 2):
         copy = pltpu.make_async_remote_copy(
             src_ref=forward.at[pl.ds(d * SPILL, SPILL)],
             dst_ref=left.at[pl.ds(SLOTS + d * SPILL, SPILL)],
             send_sem=s.spill_sems.at[0, d],
             recv_sem=s.spill_sems.at[1, d],
-            device_id=place.at(0, 0, d + 1)[2],
+            device_id=place.at(0, 0, d + 1),
             device_id_type=MESH,
         )
         copy.start()
         to_line.append(copy)
-    s.label_out[0:8] = label
-    s.label_out[8:16] = failed
-    copy_label = to_pair(s.label_out, s.label_in, 4)
-    s.places_out[...] = places.reshape(8, 1, LANES)
-    to_sources(place, s.places_out, s.places_in, s.send_sems.at[2], s.places_sem)
-
-    def set_bias(ref, tags):
-        for q in range(8):
-            ref[q * LANES : (q + 1) * LANES, 0:1] = jnp.where(column(tags, q) == own, 0.0, NONE)
-
-    def against(right, right_bias, first, count, same):
-        def one(index, best):
-            base = pl.multiple_of(index * QUARTER, QUARTER)
-            part = pl.ds(base, QUARTER)
-            scores = dot_t(right[part], left[first : first + count]) + right_bias[part, 0:1]
-            if same:
-                scores = jnp.where(
-                    iota((QUARTER, count), 0) + base == iota((QUARTER, count), 1), NONE, scores
-                )
-            return jnp.maximum(best, fold(scores))
-
-        start = jnp.full((8, count), NONE, jnp.float32)
-        return lax.fori_loop(0, SLOTS // QUARTER, one, start)
-
-    bias, other_bias = s.bias, s.other_bias
-    set_bias(bias, label)
-    best_main = against(left, bias, 0, SLOTS, True)
-    copy_label.wait()
-    set_bias(other_bias, s.label_in[0:8])
-    for copy in shared:
-        copy.wait()
-    best_main = jnp.maximum(best_main, against(other, other_bias, 0, SLOTS, False))
+    blocks(left, bias, SIDE - 1, True)
+    for phase in (SIDE - 2, SIDE - 1):
+        shared[phase].wait()
+        blocks(other, other_bias, phase, False)
+
+    rows = cluster.shape[1]
+    wait_for(s.places_in, s.places_sem)
+    held = dot(s.places_in[...].reshape(CELLS, LANES).astype(jnp.bfloat16), at_lane)
+    held = jnp.sum(held * in_cell, axis=0, keepdims=True).astype(jnp.int32)
+    straight = chip == cluster
+    entry = ENTRY * (team * 4 + cluster) + jnp.where(
+        straight, 0, 1 + (held >= LANES).astype(jnp.int32)
+    )
+    in_entry = (iota((ENTRY * CELLS, rows), 0) == entry).astype(jnp.float32)
+    spot = jnp.where(straight, lane, jnp.where(held >= LANES, held - LANES, held))
+    at_spot = (iota((LANES, rows), 0) == spot).astype(jnp.bfloat16)
 
     for copy in to_line:
         copy.wait()
     spill_pair = to_pair(left.at[pl.ds(SLOTS, FORWARD)], s.other_spill, 5)
-    best_spill = against(left, bias, SLOTS, LEFT_SPILL, False)
-    best_spill = jnp.maximum(best_spill, against(other, other_bias, SLOTS, LEFT_SPILL, False))
+
+    def against(right, right_bias, best):
+        def one(index, best):
+            part = rows_of(index)
+            scores = dot_t(right[part], left[SLOTS:]) + right_bias[part, 0:1]
+            return jnp.maximum(best, fold(scores))
+
+        return lax.fori_loop(0, SIDE, one, best)
 
     def against_spill(right, same):
         scores = dot_t(right, left[...]) + jnp.where(
@@ -364,45 +418,41 @@
             )
         return fold(scores)
 
+    best_spill = jnp.full((8, LEFT_SPILL), NONE, jnp.float32)
+    best_spill = against(left, bias, best_spill)
+    best_spill = against(other, other_bias, best_spill)
     best_all = against_spill(left[SLOTS : SLOTS + FORWARD], True)
-    rows = cluster.shape[1]
-    wait_for(s.places_in, s.places_sem)
-    held = dot(s.places_in[...].reshape(CELLS, LANES).astype(jnp.bfloat16), at_lane)
-    held = jnp.sum(held * in_cell, axis=0, keepdims=True).astype(jnp.int32)
-    at_held = (iota((LEFT_SPILL, rows), 0) == held).astype(jnp.bfloat16)
-    in_own = (iota((CELLS, rows), 0) == team * 4 + cluster).astype(jnp.float32)
     spill_pair.wait()
     best_all = jnp.maximum(best_all, against_spill(s.other_spill[...], False))
-    best_main = jnp.max(jnp.maximum(best_main, best_all[:, 0:SLOTS]), axis=0, keepdims=True)
     best_spill = jnp.max(jnp.maximum(best_spill, best_all[:, SLOTS:]), axis=0, keepdims=True)
 
     failed = jnp.maximum(failed, s.label_in[8:16])[0:1]
     best_out = s.best_out
     for q in range(8):
-        part = best_main[:, q * LANES : (q + 1) * LANES]
-        best_out[q, :, 0:LANES] = jnp.where(failed > 0.0, FAILED, part)
-        best_out[q, :, LANES:] = best_spill
-    to_sources(place, best_out, s.best_in, s.send_sems.at[3], s.best_sem)
+        half = slice((q % 2) * LANES, (q % 2 + 1) * LANES)
+        part = jnp.maximum(s.best[q // 2, :, half], best_all[:, q * LANES : (q + 1) * LANES])
+        part = jnp.max(part, axis=0, keepdims=True)
+        best_out[q * ENTRY] = jnp.where(failed > 0.0, FAILED, part)
+        for half in range(LEFT_SPILL // LANES):
+            best_out[q * ENTRY + 1 + half] = best_spill[:, half * LANES : (half + 1) * LANES]
+    to_sources(place, best_out, s.best_in, ENTRY, s.send_sems.at[3], s.best_sem)
     wait_for(s.best_in, s.best_sem)
-    found = s.best_in[...].reshape(CELLS, LANES + LEFT_SPILL)
-    worst = jnp.max(jnp.max(found, axis=1, keepdims=True), axis=0, keepdims=True)
-    straight = sum(dot(piece, at_lane) for piece in split3(found[:, 0:LANES]))
-    straight = jnp.sum(straight * in_cell, axis=0, keepdims=True)
-    moved = sum(dot(piece, at_held) for piece in split3(found[:, LANES:]))
-    moved = jnp.sum(moved * in_own, axis=0, keepdims=True)
-    score = jnp.maximum(jnp.where(chip == cluster, straight, moved), -1.0)
+    found = s.best_in[...].reshape(ENTRY * CELLS, LANES)
+    worst = jnp.max(jnp.max(found, axis=0, keepdims=True), axis=1, keepdims=True)
+    picked = sum(dot(piece, at_spot) for piece in split3(found))
+    score = jnp.maximum(jnp.sum(picked * in_entry, axis=0, keepdims=True), -1.0)
     s.out[...] = jnp.where(worst > 4.0, FAILED, score)
 
     wait_sent(s)
     sent = pl.ds(0, CELLS - 1)
     wait_for(s.places_in.at[sent], s.send_sems.at[2])
-    wait_for(s.best_in.at[sent], s.send_sems.at[3])
+    wait_for(s.best_in.at[pl.ds(0, ENTRY * (CELLS - 1))], s.send_sems.at[3])
 
 
 def general_kernel(names, *refs):
     s = types.SimpleNamespace(**dict(zip(names, refs)))
     place = Place()
-    in_cell, at_lane, _, _, _ = regroup(place, s)
+    in_cell, at_lane, *_ = regroup(place, s)
     left = s.left
     for phase in range(SIDE):
         wait_for(left.at[arrived(place, phase)], s.recv_sems.at[phase])
@@ -417,7 +467,7 @@
                 dst_ref=dst.at[block - 1],
                 send_sem=s.line_sems.at[0, index, block - 1],
                 recv_sem=s.line_sems.at[1, index, block - 1],
-                device_id=place.at(0, 0, block // 2, block % 2)[2],
+                device_id={"member": place.xs[block // 2] * 2 + (place.core + block) % 2},
                 device_id_type=MESH,
             )
             copy.start()
@@ -451,7 +501,7 @@
     best = jnp.max(lax.fori_loop(0, 7, block, best), axis=0, keepdims=True)
     for q in range(8):
         s.best_out[q] = best[:, q * LANES : (q + 1) * LANES]
-    to_sources(place, s.best_out, s.best_in, s.send_sems.at[2], s.best_sem)
+    to_sources(place, s.best_out, s.best_in, 1, s.send_sems.at[2], s.best_sem)
     wait_for(s.best_in, s.best_sem)
     found = s.best_in[...].reshape(CELLS, LANES)
     score = sum(dot(piece, at_lane) for piece in split3(found))
@@ -502,15 +552,17 @@
         left=vmem((SLOTS + LEFT_SPILL, features), bf16),
         other=vmem((SLOTS, features), bf16),
         other_spill=vmem((FORWARD, features), bf16),
-        select=vmem((FORWARD, SLOTS), bf16),
+        select=vmem((SIDE, FORWARD, QUARTER), bf16),
+        moved=vmem((FORWARD, features), f32),
+        best=vmem((SIDE, 8, QUARTER), f32),
         forward=vmem((FORWARD, features), bf16),
         label_out=vmem((16, LANES), f32),
         label_in=vmem((16, LANES), f32),
         other_bias=vmem((SLOTS, LANES), f32),
         places_out=vmem((8, 1, LANES), f32),
         places_in=vmem((CELLS, 1, LANES), f32),
-        best_out=vmem((8, 1, LANES + LEFT_SPILL), f32),
-        best_in=vmem((CELLS, 1, LANES + LEFT_SPILL), f32),
+        best_out=vmem((8 * ENTRY, 1, LANES), f32),
+        best_in=vmem((CELLS * ENTRY, 1, LANES), f32),
         places_sem=dma,
         pair_sems=dma((2, 6)),
         spill_sems=dma((2, 3)),

time: 55.4 us -> 50.9 us (0.919)
  Pallas kernels: 53.5 us -> 48.8 us
    pallas_call x1, Pallas kernels: 53.5 us -> 48.8 us  [call(): pl.pallas_call(functools.partial(kernel, names), out_shape=jax.ShapeDtype...]
where the time goes in v3:
time: 50.9 us; the launch traced here: 50.8 us
  Pallas kernels  48.8 us (96%)
  local copies, waits for them, and re-layouts  1.1 us (2%)
  between operations  0.71 us (1%)
    pallas_call x1, Pallas kernels, call(): pl.pallas_call(functools.partial(kernel, names), out_shape=jax.ShapeDtype...  48.8 us

profile of v3, /device:TPU:0, one launch (start us, length us, event | category | flops | bytes accessed | tf_op | source)
XLA Modules:
  0.0 50.8 jit_solution(7121337435069535442)
XLA Ops:
  0.0 0.0 copy-start
  0.0 0.0 copy-start.2
  0.0 48.8 %team_scores.1 = f32[1,512]{1,0:T(1,128)S(1)} custom-call(s32[1,512]{1,0:T(1,128)} %bitcast.7, s32[1,512]{1,0:T(1,128)} %bitcast.9, bf16[512,768]{1,0:T(8,128)(2,1)} %refs_2_.1), custom_call_target="tpu_custom_call" | custom-call | tf_op jit(solution)/shard_map/team_scores/pallas_call | solution.py:536
  48.8 0.5 %slice.3 = f32[1,1]{1,0:T(1,128)} slice(f32[1,512]{1,0:T(1,128)S(1)} %team_scores.1), slice={[0:1], [0:1]} | slice | bytes 8 | tf_op jit(solution)/shard_map/slice | solution.py:593
  49.3 0.0 copy-start.1
  50.0 0.0 copy-done
  50.0 0.0 copy-done.2
  50.0 0.0 copy-done.1
  50.0 0.2 conditional.1
  50.2 0.6 %copy.10 = f32[512]{0:T(512)} copy(f32[512]{0:T(512)S(1)} %get-tuple-element.18) | data formatting | bytes 4096
Async XLA Ops:
  0.0 50.0 %copy-start = (bf16[512,768]{1,0:T(8,128)(2,1)S(1)}, bf16[512,768]{1,0:T(8,128)(2,1)}, u32[]{:S(2)}) copy-start(bf16[512,768]{1,0:T(8,128)(2,1)} %refs_2_.1) | copy-start | bytes 2359300
  0.0 50.0 %copy-start.2 = (s32[512]{0:T(512)S(1)}, s32[512]{0:T(512)}, u32[]{:S(2)}) copy-start(s32[512]{0:T(512)} %param.7) | copy-start | bytes 6148
  49.3 0.7 %copy-start.1 = (s32[512]{0:T(512)S(1)}, s32[512]{0:T(512)}, u32[]{:S(2)}) copy-start(s32[512]{0:T(512)} %param.6) | copy-start | bytes 6148

commit v4 on v3

--- a/solution.py
+++ b/solution.py
@@ -23,6 +23,7 @@
 ENTRY = 3
 FAILED = 8.0
 EMPTY = 2.0
+SPILL_ORDER = (1, 0, 2)
 
 
 def split3(value):
@@ -85,19 +86,30 @@
     return [(dy, dz, (phase - dy - dz) % SIDE) for dy in range(SIDE) for dz in range(SIDE)]
 
 
-OTHERS = [offset for phase in range(SIDE) for offset in offsets(phase)][1:]
+def mixed(phase):
+    pairs = sorted(enumerate(offsets(phase)), key=lambda pair: hops(pair[1]))
+    return [pair for both in zip(pairs[:8], pairs[:7:-1]) for pair in both]
+
+
+def hops(offset):
+    return sum(min(d, SIDE - d) for d in offset)
+
+
+OTHERS = sorted(
+    [offset for phase in range(SIDE) for offset in offsets(phase)][1:],
+    key=lambda offset: -hops(offset),
+)
 
 
 def wait_for(ref, sem):
     pltpu.make_async_copy(ref, ref, sem).wait()
 
 
-def greet(place, s):
+def greet(place):
     barrier = pltpu.get_barrier_semaphore()
-    for d in range(1, SIDE):
-        for offset in ((d, 0, 0), (0, d, 0), (0, 0, d)):
-            device = place.at(*offset)
-            pl.semaphore_signal(barrier, inc=1, device_id=device, device_id_type=MESH)
+    plane = [(dy, dz, 0) for dy in range(SIDE) for dz in range(SIDE)][1:]
+    for offset in plane + [(0, 0, d) for d in range(1, SIDE)]:
+        pl.semaphore_signal(barrier, inc=1, device_id=place.at(*offset), device_id_type=MESH)
     pl.semaphore_signal(barrier, inc=1, device_id=place.sibling, device_id_type=MESH)
     return barrier
 
@@ -111,7 +123,7 @@
     ]
     for copy in load:
         copy.start()
-    barrier = greet(place, s)
+    barrier = greet(place)
     load[0].wait()
     load[1].wait()
 
@@ -159,25 +171,12 @@
     slot = lax.rem(dy + dz + dx, SIDE) * QUARTER + (dy * SIDE + dz) * CELL + spot
     lane = spot + (place.source % 8) * CELL
 
-    pl.semaphore_wait(barrier, 10)
-    for d in range(1, SIDE):
-        device = place.at(0, d, 0)
-        pl.semaphore_signal(s.line_sem, inc=1, device_id=device, device_id_type=MESH)
-
-    load[2].wait()
-    values = s.embed[...].astype(jnp.float32)
-    norm = jnp.sum(values * values, axis=1, keepdims=True)
-    s.unit[...] = (values * lax.rsqrt(norm + 1e-06)).astype(jnp.bfloat16)
-
-    pl.semaphore_wait(s.line_sem, 3)
+    pl.semaphore_wait(barrier, 19)
     for d in range(1, SIDE):
         device = place.at(0, 0, d)
         pl.semaphore_signal(s.plane_sem, inc=1, device_id=device, device_id_type=MESH)
 
-    in_cell = (iota((CELLS, rows), 0) == cell).astype(jnp.float32)
-    at_lane = (iota((LANES, rows), 0) == lane).astype(jnp.bfloat16)
-    labels = (in_cell * (cluster + 1).astype(jnp.float32)).astype(jnp.bfloat16)
-    s.meta[...] = dot_t(labels, at_lane).reshape(CELLS, 1, LANES)
+    load[2].wait()
 
     send, left = s.send, s.left
 
@@ -187,14 +186,17 @@
     for phase in range(SIDE):
         base = phase * QUARTER
         chosen = (iota((QUARTER, rows), 0) + base == slot).astype(jnp.bfloat16)
-        send[base : base + QUARTER] = dot(chosen, s.unit[...]).astype(jnp.bfloat16)
+        values = dot(chosen, s.embed[...])
+        norm = jnp.sum(values * values, axis=1, keepdims=True)
+        unit = (values * lax.rsqrt(norm + 1e-06)).astype(jnp.bfloat16)
+        send[base : base + QUARTER] = unit
         if phase == 0:
             pl.semaphore_wait(s.plane_sem, 3)
             pltpu.make_async_copy(
                 send.at[pl.ds(0, CELL)], left.at[landing(place.source)], s.recv_sems.at[0]
             ).start()
 
-        for index, offset in enumerate(offsets(phase)):
+        for index, offset in mixed(phase):
             if any(offset):
                 pltpu.make_async_remote_copy(
                     src_ref=send.at[landing(phase * 16 + index)],
@@ -205,6 +207,10 @@
                     device_id_type=MESH,
                 ).start()
         if phase == META_AFTER:
+            in_cell = (iota((CELLS, rows), 0) == cell).astype(jnp.float32)
+            at_lane = (iota((LANES, rows), 0) == lane).astype(jnp.bfloat16)
+            labels = (in_cell * (cluster + 1).astype(jnp.float32)).astype(jnp.bfloat16)
+            s.meta[...] = dot_t(labels, at_lane).reshape(CELLS, 1, LANES)
             send_labels(place, s)
     return in_cell, at_lane, team, cluster, chip, lane
 
@@ -368,7 +374,7 @@
 
     forward[...] = s.moved[...].astype(jnp.bfloat16)
     to_line = []
-    for d in (1, 0, 2):
+    for d in SPILL_ORDER:
         copy = pltpu.make_async_remote_copy(
             src_ref=forward.at[pl.ds(d * SPILL, SPILL)],
             dst_ref=left.at[pl.ds(SLOTS + d * SPILL, SPILL)],
@@ -396,9 +402,13 @@
     spot = jnp.where(straight, lane, jnp.where(held >= LANES, held - LANES, held))
     at_spot = (iota((LANES, rows), 0) == spot).astype(jnp.bfloat16)
 
-    for copy in to_line:
+    spill_pair = []
+    for d, copy in zip(SPILL_ORDER, to_line):
         copy.wait()
-    spill_pair = to_pair(left.at[pl.ds(SLOTS, FORWARD)], s.other_spill, 5)
+        part = pl.ds(d * SPILL, SPILL)
+        spill_pair.append(
+            to_pair(left.at[pl.ds(SLOTS + d * SPILL, SPILL)], s.other_spill.at[part], 5 + d)
+        )
 
     def against(right, right_bias, best):
         def one(index, best):
@@ -422,7 +432,8 @@
     best_spill = against(left, bias, best_spill)
     best_spill = against(other, other_bias, best_spill)
     best_all = against_spill(left[SLOTS : SLOTS + FORWARD], True)
-    spill_pair.wait()
+    for copy in spill_pair:
+        copy.wait()
     best_all = jnp.maximum(best_all, against_spill(s.other_spill[...], False))
     best_spill = jnp.max(jnp.maximum(best_spill, best_all[:, SLOTS:]), axis=0, keepdims=True)
 
@@ -436,6 +447,8 @@
         for half in range(LEFT_SPILL // LANES):
             best_out[q * ENTRY + 1 + half] = best_spill[:, half * LANES : (half + 1) * LANES]
     to_sources(place, best_out, s.best_in, ENTRY, s.send_sems.at[3], s.best_sem)
+    wait_sent(s)
+    wait_for(s.places_in.at[pl.ds(0, CELLS - 1)], s.send_sems.at[2])
     wait_for(s.best_in, s.best_sem)
     found = s.best_in[...].reshape(ENTRY * CELLS, LANES)
     worst = jnp.max(jnp.max(found, axis=0, keepdims=True), axis=1, keepdims=True)
@@ -443,9 +456,6 @@
     score = jnp.maximum(jnp.sum(picked * in_entry, axis=0, keepdims=True), -1.0)
     s.out[...] = jnp.where(worst > 4.0, FAILED, score)
 
-    wait_sent(s)
-    sent = pl.ds(0, CELLS - 1)
-    wait_for(s.places_in.at[sent], s.send_sems.at[2])
     wait_for(s.best_in.at[pl.ds(0, ENTRY * (CELLS - 1))], s.send_sems.at[3])
 
 
@@ -518,12 +528,10 @@
         dest=vmem((1, rows), i32),
         cluster=vmem((1, rows), i32),
         embed=vmem((rows, features), bf16),
-        unit=vmem((rows, features), bf16),
         send=vmem((SLOTS, features), bf16),
         meta=vmem((CELLS, 1, LANES), f32),
         meta_in=vmem((CELLS, 1, LANES), f32),
         bias=vmem((SLOTS, LANES), f32),
-        line_sem=pltpu.SemaphoreType.REGULAR,
         plane_sem=pltpu.SemaphoreType.REGULAR,
         load_sems=dma((3,)),
         send_sems=dma((4,)),
@@ -564,7 +572,7 @@
         best_out=vmem((8 * ENTRY, 1, LANES), f32),
         best_in=vmem((CELLS * ENTRY, 1, LANES), f32),
         places_sem=dma,
-        pair_sems=dma((2, 6)),
+        pair_sems=dma((2, 8)),
         spill_sems=dma((2, 3)),
     )
 

time: 50.9 us -> 49.8 us (0.978)
  Pallas kernels: 48.8 us -> 47.7 us
    pallas_call x1, Pallas kernels: 48.8 us -> 47.7 us  [call(): pl.pallas_call(functools.partial(kernel, names), out_shape=jax.ShapeDtype...]
where the time goes in v4:
time: 49.8 us; the launch traced here: 49.7 us
  Pallas kernels  47.7 us (96%)
  local copies, waits for them, and re-layouts  1.1 us (2%)
  between operations  0.71 us (1%)
    pallas_call x1, Pallas kernels, call(): pl.pallas_call(functools.partial(kernel, names), out_shape=jax.ShapeDtype...  47.7 us

profile of v4, /device:TPU:0, one launch (start us, length us, event | category | flops | bytes accessed | tf_op | source)
XLA Modules:
  0.0 49.7 jit_solution(5683530263329196890)
XLA Ops:
  0.0 0.0 copy-start
  0.0 0.0 copy-start.2
  0.0 47.7 %team_scores.1 = f32[1,512]{1,0:T(1,128)S(1)} custom-call(s32[1,512]{1,0:T(1,128)} %bitcast.7, s32[1,512]{1,0:T(1,128)} %bitcast.9, bf16[512,768]{1,0:T(8,128)(2,1)} %refs_2_.1), custom_call_target="tpu_custom_call" | custom-call | tf_op jit(solution)/shard_map/team_scores/pallas_call | solution.py:544
  47.7 0.5 %slice.3 = f32[1,1]{1,0:T(1,128)} slice(f32[1,512]{1,0:T(1,128)S(1)} %team_scores.1), slice={[0:1], [0:1]} | slice | bytes 8 | tf_op jit(solution)/shard_map/slice | solution.py:601
  48.2 0.0 copy-start.1
  48.9 0.0 copy-done
  48.9 0.0 copy-done.2
  48.9 0.0 copy-done.1
  48.9 0.2 conditional.1
  49.1 0.6 %copy.10 = f32[512]{0:T(512)} copy(f32[512]{0:T(512)S(1)} %get-tuple-element.18) | data formatting | bytes 4096
Async XLA Ops:
  0.0 48.9 %copy-start = (bf16[512,768]{1,0:T(8,128)(2,1)S(1)}, bf16[512,768]{1,0:T(8,128)(2,1)}, u32[]{:S(2)}) copy-start(bf16[512,768]{1,0:T(8,128)(2,1)} %refs_2_.1) | copy-start | bytes 2359300
  0.0 48.9 %copy-start.2 = (s32[512]{0:T(512)S(1)}, s32[512]{0:T(512)}, u32[]{:S(2)}) copy-start(s32[512]{0:T(512)} %param.7) | copy-start | bytes 6148
  48.2 0.7 %copy-start.1 = (s32[512]{0:T(512)S(1)}, s32[512]{0:T(512)}, u32[]{:S(2)}) copy-start(s32[512]{0:T(512)} %param.6) | copy-start | bytes 6148

commit v5 on v4

--- a/solution.py
+++ b/solution.py
@@ -411,12 +411,7 @@
         )
 
     def against(right, right_bias, best):
-        def one(index, best):
-            part = rows_of(index)
-            scores = dot_t(right[part], left[SLOTS:]) + right_bias[part, 0:1]
-            return jnp.maximum(best, fold(scores))
-
-        return lax.fori_loop(0, SIDE, one, best)
+        return jnp.maximum(best, fold(dot_t(right[0:SLOTS], left[SLOTS:]) + right_bias[:, 0:1]))
 
     def against_spill(right, same):
         scores = dot_t(right, left[...]) + jnp.where(
@@ -428,10 +423,8 @@
             )
         return fold(scores)
 
-    best_spill = jnp.full((8, LEFT_SPILL), NONE, jnp.float32)
-    best_spill = against(left, bias, best_spill)
-    best_spill = against(other, other_bias, best_spill)
     best_all = against_spill(left[SLOTS : SLOTS + FORWARD], True)
+    best_spill = against(other, other_bias, against(left, bias, best_all[:, SLOTS:]))
     for copy in spill_pair:
         copy.wait()
     best_all = jnp.maximum(best_all, against_spill(s.other_spill[...], False))
@@ -439,11 +432,11 @@
 
     failed = jnp.maximum(failed, s.label_in[8:16])[0:1]
     best_out = s.best_out
+    best_main = jnp.concatenate([s.best[q] for q in range(SIDE)], axis=1)
+    best_main = jnp.max(jnp.maximum(best_main, best_all[:, 0:SLOTS]), axis=0, keepdims=True)
+    best_main = jnp.where(failed[0:1, 0:1] > 0.0, FAILED, best_main)
     for q in range(8):
-        half = slice((q % 2) * LANES, (q % 2 + 1) * LANES)
-        part = jnp.maximum(s.best[q // 2, :, half], best_all[:, q * LANES : (q + 1) * LANES])
-        part = jnp.max(part, axis=0, keepdims=True)
-        best_out[q * ENTRY] = jnp.where(failed > 0.0, FAILED, part)
+        best_out[q * ENTRY] = best_main[:, q * LANES : (q + 1) * LANES]
         for half in range(LEFT_SPILL // LANES):
             best_out[q * ENTRY + 1 + half] = best_spill[:, half * LANES : (half + 1) * LANES]
     to_sources(place, best_out, s.best_in, ENTRY, s.send_sems.at[3], s.best_sem)

time: 49.8 us -> 48.4 us (0.972)
  Pallas kernels: 47.7 us -> 46 us
    pallas_call x1, Pallas kernels: 47.7 us -> 46 us  [call(): pl.pallas_call(functools.partial(kernel, names), out_shape=jax.ShapeDtype...]
where the time goes in v5:
time: 48.4 us; the launch traced here: 48 us
  Pallas kernels  46 us (95%)
  local copies, waits for them, and re-layouts  1.1 us (2%)
  between operations  0.71 us (1%)
    pallas_call x1, Pallas kernels, call(): pl.pallas_call(functools.partial(kernel, names), out_shape=jax.ShapeDtype...  46 us

profile of v5, /device:TPU:0, one launch (start us, length us, event | category | flops | bytes accessed | tf_op | source)
XLA Modules:
  0.0 48.0 jit_solution(12576614831822261329)
XLA Ops:
  0.0 0.0 copy-start
  0.0 0.0 copy-start.2
  0.0 46.0 %team_scores.1 = f32[1,512]{1,0:T(1,128)S(1)} custom-call(s32[1,512]{1,0:T(1,128)} %bitcast.7, s32[1,512]{1,0:T(1,128)} %bitcast.9, bf16[512,768]{1,0:T(8,128)(2,1)} %refs_2_.1), custom_call_target="tpu_custom_call" | custom-call | tf_op jit(solution)/shard_map/team_scores/pallas_call | solution.py:537
  46.0 0.5 %slice.3 = f32[1,1]{1,0:T(1,128)} slice(f32[1,512]{1,0:T(1,128)S(1)} %team_scores.1), slice={[0:1], [0:1]} | slice | bytes 8 | tf_op jit(solution)/shard_map/slice | solution.py:594
  46.5 0.0 copy-start.1
  47.2 0.0 copy-done
  47.2 0.0 copy-done.2
  47.2 0.0 copy-done.1
  47.2 0.2 conditional.1
  47.4 0.6 %copy.10 = f32[512]{0:T(512)} copy(f32[512]{0:T(512)S(1)} %get-tuple-element.18) | data formatting | bytes 4096
Async XLA Ops:
  0.0 47.2 %copy-start = (bf16[512,768]{1,0:T(8,128)(2,1)S(1)}, bf16[512,768]{1,0:T(8,128)(2,1)}, u32[]{:S(2)}) copy-start(bf16[512,768]{1,0:T(8,128)(2,1)} %refs_2_.1) | copy-start | bytes 2359300
  0.0 47.2 %copy-start.2 = (s32[512]{0:T(512)S(1)}, s32[512]{0:T(512)}, u32[]{:S(2)}) copy-start(s32[512]{0:T(512)} %param.7) | copy-start | bytes 6148
  46.5 0.7 %copy-start.1 = (s32[512]{0:T(512)S(1)}, s32[512]{0:T(512)}, u32[]{:S(2)}) copy-start(s32[512]{0:T(512)} %param.6) | copy-start | bytes 6148

commit v6 on v5

--- a/solution.py
+++ b/solution.py
@@ -19,7 +19,7 @@
 FORWARD = 3 * SPILL
 LEFT_SPILL = 256
 NONE = -4.0
-META_AFTER = 0
+LABELS_AT = (0, 8)
 ENTRY = 3
 FAILED = 8.0
 EMPTY = 2.0
@@ -196,7 +196,13 @@
                 send.at[pl.ds(0, CELL)], left.at[landing(place.source)], s.recv_sems.at[0]
             ).start()
 
-        for index, offset in mixed(phase):
+        for count, (index, offset) in enumerate(mixed(phase)):
+            if (phase, count) == LABELS_AT:
+                in_cell = (iota((CELLS, rows), 0) == cell).astype(jnp.float32)
+                at_lane = (iota((LANES, rows), 0) == lane).astype(jnp.bfloat16)
+                labels = (in_cell * (cluster + 1).astype(jnp.float32)).astype(jnp.bfloat16)
+                s.meta[...] = dot_t(labels, at_lane).reshape(CELLS, 1, LANES)
+                send_labels(place, s)
             if any(offset):
                 pltpu.make_async_remote_copy(
                     src_ref=send.at[landing(phase * 16 + index)],
@@ -206,12 +212,6 @@
                     device_id=place.at(*offset),
                     device_id_type=MESH,
                 ).start()
-        if phase == META_AFTER:
-            in_cell = (iota((CELLS, rows), 0) == cell).astype(jnp.float32)
-            at_lane = (iota((LANES, rows), 0) == lane).astype(jnp.bfloat16)
-            labels = (in_cell * (cluster + 1).astype(jnp.float32)).astype(jnp.bfloat16)
-            s.meta[...] = dot_t(labels, at_lane).reshape(CELLS, 1, LANES)
-            send_labels(place, s)
     return in_cell, at_lane, team, cluster, chip, lane
 
 
@@ -372,9 +372,10 @@
                 shared[phase - 1].wait()
                 blocks(other, other_bias, phase - 1, False)
 
-    forward[...] = s.moved[...].astype(jnp.bfloat16)
     to_line = []
     for d in SPILL_ORDER:
+        part = slice(d * SPILL, (d + 1) * SPILL)
+        forward[part] = s.moved[part].astype(jnp.bfloat16)
         copy = pltpu.make_async_remote_copy(
             src_ref=forward.at[pl.ds(d * SPILL, SPILL)],
             dst_ref=left.at[pl.ds(SLOTS + d * SPILL, SPILL)],

time: 48.4 us -> 48.2 us (level)
  no operation moved by 1% of the time
where the time goes in v6:
time: 48.2 us; the launch traced here: 47.9 us
  Pallas kernels  45.9 us (95%)
  local copies, waits for them, and re-layouts  1.1 us (2%)
  between operations  0.71 us (1%)
    pallas_call x1, Pallas kernels, call(): pl.pallas_call(functools.partial(kernel, names), out_shape=jax.ShapeDtype...  45.9 us

profile of v6, /device:TPU:0, one launch (start us, length us, event | category | flops | bytes accessed | tf_op | source)
XLA Modules:
  0.0 47.9 jit_solution(2225052866743260591)
XLA Ops:
  0.0 0.0 copy-start
  0.0 0.0 copy-start.2
  0.0 45.9 %team_scores.1 = f32[1,512]{1,0:T(1,128)S(1)} custom-call(s32[1,512]{1,0:T(1,128)} %bitcast.7, s32[1,512]{1,0:T(1,128)} %bitcast.9, bf16[512,768]{1,0:T(8,128)(2,1)} %refs_2_.1), custom_call_target="tpu_custom_call" | custom-call | tf_op jit(solution)/shard_map/team_scores/pallas_call | solution.py:538
  45.9 0.5 %slice.3 = f32[1,1]{1,0:T(1,128)} slice(f32[1,512]{1,0:T(1,128)S(1)} %team_scores.1), slice={[0:1], [0:1]} | slice | bytes 8 | tf_op jit(solution)/shard_map/slice | solution.py:595
  46.4 0.0 copy-start.1
  47.1 0.0 copy-done
  47.1 0.0 copy-done.2
  47.1 0.0 copy-done.1
  47.1 0.2 conditional.1
  47.3 0.6 %copy.10 = f32[512]{0:T(512)} copy(f32[512]{0:T(512)S(1)} %get-tuple-element.18) | data formatting | bytes 4096
Async XLA Ops:
  0.0 47.1 %copy-start = (bf16[512,768]{1,0:T(8,128)(2,1)S(1)}, bf16[512,768]{1,0:T(8,128)(2,1)}, u32[]{:S(2)}) copy-start(bf16[512,768]{1,0:T(8,128)(2,1)} %refs_2_.1) | copy-start | bytes 2359300
  0.0 47.1 %copy-start.2 = (s32[512]{0:T(512)S(1)}, s32[512]{0:T(512)}, u32[]{:S(2)}) copy-start(s32[512]{0:T(512)} %param.7) | copy-start | bytes 6148
  46.4 0.7 %copy-start.1 = (s32[512]{0:T(512)S(1)}, s32[512]{0:T(512)}, u32[]{:S(2)}) copy-start(s32[512]{0:T(512)} %param.6) | copy-start | bytes 6148

commit v7 on v5

--- a/solution.py
+++ b/solution.py
@@ -385,10 +385,22 @@
         )
         copy.start()
         to_line.append(copy)
-    blocks(left, bias, SIDE - 1, True)
-    for phase in (SIDE - 2, SIDE - 1):
-        shared[phase].wait()
-        blocks(other, other_bias, phase, False)
+    last = quarter(place, SIDE - 1)
+
+    def last_blocks(right, right_bias, same):
+        scores = dot_t(right[0:SLOTS], left[rows_of(last)]) + right_bias[:, 0:1]
+        if same:
+            shape = (SLOTS, QUARTER)
+            scores = jnp.where(iota(shape, 0) == iota(shape, 1) + last * QUARTER, NONE, scores)
+        s.best[last] = jnp.maximum(s.best[last], fold(scores))
+        for phase in range(SIDE - 1):
+            block(right, right_bias, last, quarter(place, phase))
+
+    last_blocks(left, bias, True)
+    shared[SIDE - 2].wait()
+    blocks(other, other_bias, SIDE - 2, False)
+    shared[SIDE - 1].wait()
+    last_blocks(other, other_bias, False)
 
     rows = cluster.shape[1]
     wait_for(s.places_in, s.places_sem)

time: 48.4 us -> 48.4 us (level)
  no operation moved by 1% of the time
where the time goes in v7:
time: 48.4 us; the launch traced here: 47.9 us
  Pallas kernels  45.9 us (95%)
  local copies, waits for them, and re-layouts  1.1 us (2%)
  between operations  0.71 us (1%)
    pallas_call x1, Pallas kernels, call(): pl.pallas_call(functools.partial(kernel, names), out_shape=jax.ShapeDtype...  45.9 us

profile of v7, /device:TPU:0, one launch (start us, length us, event | category | flops | bytes accessed | tf_op | source)
XLA Modules:
  0.0 47.9 jit_solution(7978122782086885045)
XLA Ops:
  0.0 0.0 copy-start
  0.0 0.0 copy-start.2
  0.0 45.9 %team_scores.1 = f32[1,512]{1,0:T(1,128)S(1)} custom-call(s32[1,512]{1,0:T(1,128)} %bitcast.7, s32[1,512]{1,0:T(1,128)} %bitcast.9, bf16[512,768]{1,0:T(8,128)(2,1)} %refs_2_.1), custom_call_target="tpu_custom_call" | custom-call | tf_op jit(solution)/shard_map/team_scores/pallas_call | solution.py:549
  46.0 0.5 %slice.3 = f32[1,1]{1,0:T(1,128)} slice(f32[1,512]{1,0:T(1,128)S(1)} %team_scores.1), slice={[0:1], [0:1]} | slice | bytes 8 | tf_op jit(solution)/shard_map/slice | solution.py:606
  46.5 0.0 copy-start.1
  47.1 0.0 copy-done
  47.1 0.0 copy-done.2
  47.2 0.0 copy-done.1
  47.2 0.2 conditional.1
  47.4 0.6 %copy.10 = f32[512]{0:T(512)} copy(f32[512]{0:T(512)S(1)} %get-tuple-element.18) | data formatting | bytes 4096
Async XLA Ops:
  0.0 47.1 %copy-start = (bf16[512,768]{1,0:T(8,128)(2,1)S(1)}, bf16[512,768]{1,0:T(8,128)(2,1)}, u32[]{:S(2)}) copy-start(bf16[512,768]{1,0:T(8,128)(2,1)} %refs_2_.1) | copy-start | bytes 2359300
  0.0 47.1 %copy-start.2 = (s32[512]{0:T(512)S(1)}, s32[512]{0:T(512)}, u32[]{:S(2)}) copy-start(s32[512]{0:T(512)} %param.7) | copy-start | bytes 6148
  46.5 0.7 %copy-start.1 = (s32[512]{0:T(512)S(1)}, s32[512]{0:T(512)}, u32[]{:S(2)}) copy-start(s32[512]{0:T(512)} %param.6) | copy-start | bytes 6148
